TPU v7x, 128 devices: a whole 4x4x4 slice. The times are simulated.
128 devices in a mesh: gz: 2 (over core), xy: 64 (over y, z, x).
Axes of the slice: x: 4, y: 4, z: 4, core: 2. Of those that a mesh axis runs over, the one named last changes fastest.
Arguments:
- image: bfloat16 [2, 64, 4, 1, 128, 512], P('gz', 'xy'), may hold values from -6 to 6
- bricks: bfloat16 [2, 64, 4, 1, 128, 1000], P('gz', 'xy'), may hold values from -6 to 6
- owner: int32 [2, 64, 4, 1, 128, 1], P('gz', 'xy'), may hold values from 0 to 127; in each aligned block of 512 rows (0 to 511, 512 to 1023, ..., all dimensions but the last counted through in order) at most 16 rows name the same one
- brick_index: int32 [2, 64, 4, 1, 128], P('gz', 'xy'), may hold values from 0 to 511
- offset_class: int32 [2, 64, 4, 1, 128], P('gz', 'xy'), may hold values from 0 to 63
Outputs:
- nodes: float32 [9, 8, 64, 128], P(None, 'gz', 'xy')
- gram: float32 [2, 64, 4, 1, 128, 576], P('gz', 'xy')
Inputs may be any that keep to these rules, and one draw needn't show every extreme that they name: At most 16 elements of one device take bricks from one owner, and in some device's block one owner is named by exactly 16 elements.
All inputs are finite; a program needn't handle non-finite values.
Results may differ from a plain program's by a relative error of at most 0.0025.
Values may be sent and summed in bfloat16 or wider, within the bound.
A program may use at most 128 MiB of HBM per device.

v0:
```python
import math

import jax
import jax.numpy as jnp
from jax import lax
from jax.sharding import PartitionSpec as P


def passed_along(x, axis, by):
    size = lax.axis_size(axis)
    pairs = [(i, i + by) for i in range(size) if 0 <= i + by < size]
    return lax.ppermute(x, axis, pairs)


def corner_fractions(offset):
    frac_z = ((offset // 16).astype(jnp.float32) + 0.5) / 4.0
    frac_x = ((offset // 4 % 4).astype(jnp.float32) + 0.5) / 4.0
    frac_y = ((offset % 4).astype(jnp.float32) + 0.5) / 4.0
    return (frac_z, frac_x, frac_y)


def deformed_samples(brick_rows, offset):
    cube = brick_rows.astype(jnp.float32).reshape(-1, 10, 10, 10)
    frac_z, frac_x, frac_y = corner_fractions(offset)
    total = jnp.zeros((cube.shape[0], 9, 9, 9), jnp.float32)
    for z_increment in (0, 1):
        weight_z = frac_z if z_increment else 1.0 - frac_z
        for step_x in (0, 1):
            weight_x = frac_x if step_x else 1.0 - frac_x
            for step_y in (0, 1):
                weight_y = frac_y if step_y else 1.0 - frac_y
                weight = (weight_z * weight_x * weight_y)[:, None, None, None]
                total = (
                    total
                    + weight
                    * cube[
                        :, z_increment : z_increment + 9, step_x : step_x + 9, step_y : step_y + 9
                    ]
                )
    return total.reshape(-1, 729).astype(jnp.bfloat16)


def shape_table():
    centre = (jnp.arange(8, dtype=jnp.float32) + 0.5) / 8.0
    rows = []
    for node_z in (0, 1):
        along_z = centre if node_z else 1.0 - centre
        for node_x in (0, 1):
            x_direction_shape = centre if node_x else 1.0 - centre
            for node_y in (0, 1):
                y_direction_shape = centre if node_y else 1.0 - centre
                rows.append(
                    (
                        along_z[:, None, None]
                        * x_direction_shape[None, :, None]
                        * y_direction_shape[None, None, :]
                    ).reshape(512)
                )
    return jnp.stack(rows)


def element_terms(samples, image):
    cube = samples.astype(jnp.float32).reshape(-1, 9, 9, 9)
    base = cube[:, :8, :8, :8]
    residual_values = (base - image.astype(jnp.float32).reshape(-1, 8, 8, 8)).reshape(-1, 512)
    slopes = jnp.stack(
        [cube[:, 1:, :8, :8] - base, cube[:, :8, 1:, :8] - base, cube[:, :8, :8, 1:] - base], axis=1
    )
    slopes = slopes.reshape(-1, 3, 1, 512)
    jacobian_matrix = (slopes * shape_table()[None, None, :, :]).reshape(-1, 24, 512)
    gram = (
        jnp.einsum(
            "hqy,hjy->hqj", jacobian_matrix, jacobian_matrix, precision=lax.Precision.HIGHEST
        )
        / 64.0
    )
    residual_vector = (
        jnp.einsum("xeu,xu->xe", jacobian_matrix, residual_values, precision=lax.Precision.HIGHEST)
        / 64.0
    )
    blocks = jnp.diagonal(gram.reshape(-1, 3, 8, 3, 8), axis1=2, axis2=4)
    pairs = jnp.stack(
        [
            blocks[:, 0, 0],
            blocks[:, 0, 1],
            blocks[:, 0, 2],
            blocks[:, 1, 1],
            blocks[:, 1, 2],
            blocks[:, 2, 2],
        ],
        axis=1,
    )
    node_terms = jnp.concatenate([residual_vector.reshape(-1, 3, 8), pairs], axis=1)
    return (node_terms, gram.reshape(-1, 576))


def per_device(image, bricks, owner, brick_index, offset_class):
    depth, across, along = (image.shape[2], image.shape[3], image.shape[4])
    count = depth * across * along
    layers = lax.axis_size("gz")
    columns = lax.axis_size("xy")
    devices = layers * columns
    cap = 4 * count // devices
    owner_flat = owner.reshape(count)
    wanted = brick_index.reshape(count)
    classes = offset_class.reshape(count)
    positions = jnp.arange(count, dtype=jnp.int32)
    same_owner = (owner_flat[:, None] == owner_flat[None, :]) & (
        positions[None, :] < positions[:, None]
    )
    slot = jnp.sum(same_owner.astype(jnp.int32), axis=1)
    target = owner_flat * cap + slot
    places = jnp.arange(devices * cap, dtype=jnp.int32)
    onehot = (target[:, None] == places[None, :]).astype(jnp.int32)
    want_ids = jnp.sum(onehot * wanted[:, None], axis=0).reshape(devices, cap)
    want_classes = jnp.sum(onehot * classes[:, None], axis=0).reshape(devices, cap)
    local_bricks = bricks.reshape(count, 1000)
    req_ids = (
        lax.all_to_all(want_ids, ("gz", "xy"), split_axis=0, concat_axis=0, tiled=True),
        lax.all_to_all(want_classes, ("gz", "xy"), split_axis=0, concat_axis=0, tiled=True),
    )[0]
    lead = req_ids.shape
    rows = jnp.take(local_bricks, req_ids.reshape(-1), axis=0)
    received_bricks = lax.all_to_all(
        rows.reshape(lead + (rows.shape[-1],)),
        ("gz", "xy"),
        split_axis=0,
        concat_axis=0,
        tiled=True,
    )
    received_bricks = received_bricks.reshape(devices * cap, -1)
    rows = jnp.take(received_bricks, target, axis=0)
    samples = deformed_samples(rows, classes)
    block = math.gcd(count, 512)

    def run(items):
        return element_terms(items[0], items[1])

    node_terms, gram = lax.map(
        run, (samples.reshape(-1, block, 729), image.reshape(-1, block, 512))
    )
    terms = jnp.transpose(node_terms.reshape(depth, across, along, 9, 8), (3, 4, 0, 1, 2))
    grid = jnp.zeros((9, depth + 1, across + 1, along), jnp.float32)
    for node in range(8):
        node_z, node_x, node_y = (node // 4, node // 2 % 2, node % 2)
        piece = terms[:, node]
        if node_y:
            piece = jnp.concatenate([jnp.zeros_like(piece[..., :1]), piece[..., :-1]], axis=3)
        grid = grid + jnp.pad(piece, ((0, 0), (node_z, 1 - node_z), (node_x, 1 - node_x), (0, 0)))
    face = passed_along(grid[:, :, across, :], "xy", 1)
    owned = grid[:, :, :across, :].at[:, :, 0, :].add(face)
    lid = passed_along(owned[:, depth, :, :], "gz", 1)
    nodes = owned[:, :depth, :, :].at[:, 0, :, :].add(lid)
    return (nodes, gram.reshape(1, 1, depth, across, along, 576))


def solution(mesh):
    in_specs = (
        P("gz", "xy", None, None, None, None),
        P("gz", "xy", None, None, None, None),
        P("gz", "xy", None, None, None, None),
        P("gz", "xy", None, None, None),
        P("gz", "xy", None, None, None),
    )
    out_specs = (P(None, "gz", "xy", None), P("gz", "xy", None, None, None, None))
    return jax.shard_map(
        per_device, mesh=mesh, in_specs=in_specs, out_specs=out_specs, check_vma=False
    )
```

profile of v0, /device:TPU:9, one launch (start us, length us, event | category | flops | bytes accessed | tf_op | source)
XLA Modules:
  0.0 176.7 jit_solution(12223123699992250533)
XLA Ops:
  0.6 1.0 convert_reduce_fusion
  1.6 0.7 compare_and_fusion.1
  2.3 1.2 select_reduce_fusion
  3.6 0.7 all_to_all.9
  4.3 10.8 %all-to-all-start = ((s32[128,1,16]{2,1,0:T(1,128)}), s32[128,1,16]{2,1,0:T(1,128)S(1)}, u32[]{:S(2)}, u32[]{:S(2)}) async-start(s32[128,1,16]{2,1,0:T(1,128)} %bitcast.4), calls=%async_computation | async-start | bytes 131072 | tf_op jit(solution)/shard_map/all_to_all | solution.py:119
  15.0 1.5 copy.76
  16.6 6.7 %all-to-all-done = s32[128,1,16]{2,1,0:T(1,128)S(1)} async-done(((s32[128,1,16]{2,1,0:T(1,128)}), s32[128,1,16]{2,1,0:T(1,128)S(1)}, u32[]{:S(2)}, u32[]{:S(2)}) %all-to-all-start) | async-done | bytes 8224 | tf_op jit(solution)/shard_map/all_to_all | solution.py:119
  23.3 0.5 broadcast.1285
  23.8 0.8 reduce.9
  24.6 0.1 reshape.788
  24.8 9.7 %gather_fusion = bf16[2048,1000]{1,0:T(8,128)(2,1)} fusion(bf16[512,1000]{1,0:T(8,128)(2,1)S(1)} %bitcast.106, s32[2048]{0:T(1024)S(1)} %broadcast_clamp_fusion), kind=kCustom, calls=%fused_computation | custom fusion | bytes 8200192 | tf_op jit(solution)/shard_map/jit(_take)/gather | solution.py:123
  34.4 3.8 %broadcast_select_fusion = bf16[128,16,1000]{2,1,0:T(8,128)(2,1)} fusion(bf16[128,16,1000]{2,1,0:T(8,128)(2,1)} %bitcast.108, pred[128,16]{1,0:T(8,128)(4,1)S(1)} %compare_and_fusion), kind=kLoop, calls=%fused_computation.12 | loop fusion | flops 2048000 | bytes 8194048 | tf_op jit(solution)/shard_map/jit(_take)/select_n | solution.py:123
  38.3 6.7 %all-to-all-start.1 = ((bf16[128,16,1000]{2,1,0:T(8,128)(2,1)}), bf16[128,16,1000]{2,1,0:T(8,128)(2,1)}, u32[]{:S(2)}, u32[]{:S(2)}) async-start(bf16[128,16,1000]{2,1,0:T(8,128)(2,1)} %broadcast_select_fusion), calls=%async_computation.1 | async-start | bytes 8388608 | tf_op jit(solution)/shard_map/all_to_all | solution.py:124
  45.0 0.3 copy.79
  45.3 0.4 reshape.795
  45.8 0.1 broadcast_multiply_fusion.8
  45.9 0.1 mul.617
  46.1 0.1 mul.625
  46.2 0.1 mul.627
  46.2 0.1 mul.632
  46.3 0.1 mul.634
  46.4 0.1 mul.638
  46.5 0.1 mul.640
  46.8 50.3 %all-to-all-done.1 = bf16[128,16,1000]{2,1,0:T(8,128)(2,1)} async-done(((bf16[128,16,1000]{2,1,0:T(8,128)(2,1)}), bf16[128,16,1000]{2,1,0:T(8,128)(2,1)}, u32[]{:S(2)}, u32[]{:S(2)}) %all-to-all-start.1) | async-done | bytes 4096032 | tf_op jit(solution)/shard_map/all_to_all | solution.py:124
  97.1 5.5 %gather_fusion.1 = bf16[512,1000]{1,0:T(8,128)(2,1)S(1)} fusion(bf16[2048,1000]{1,0:T(8,128)(2,1)} %bitcast.9, s32[1024]{0:T(1024)S(1)} %pad_clamp_fusion), kind=kCustom, calls=%fused_computation.1 | custom fusion | bytes 2050048 | tf_op jit(solution)/shard_map/jit(_take)/gather | solution.py:132
  102.6 1.3 copy.77
  103.9 2.2 %gather.20 = bf16[512,10,10,10]{0,3,2,1:T(8,128)(2,1)S(1)} reshape(bf16[512,1000]{0,1:T(8,128)(2,1)} %copy.77) | data formatting | bytes 2048000 | tf_op jit(solution)/shard_map/jit(_take)/gather | solution.py:132
  106.0 0.2 select_convert_fusion
  106.3 3.0 %fusion.14 = f32[512,9,9,9]{0,3,2,1:T(8,128)S(1)} fusion(f32[512,10,10,10]{0,3,2,1:T(8,128)S(1)} %select_convert_fusion, f32[512]{0:T(512)S(1)} %get-tuple-element.84, f32[512]{0:T(512)S(1)} %get-tuple-element.86, f32[512]{0:T(512)S(1)} %get-tuple-element.82, f32[512]{0:T(512)S(1)} %get-tuple-element.85, f32[512]{0:T(512)S(1)} %get-tuple-element.83, ...), kind=kLoop, calls=%fused_computation.32 | loop fusion | flops 6345216 | bytes 13453312 | tf_op jit(solution)/shard_map/while/body/eval_jaxpr/convert_element_type | solution.py:63
  109.3 2.1 %slice_subtract_fusion.2 = (f32[512,8,8,8]{0,3,2,1:T(8,128)}, f32[512,8,8,8]{0,3,2,1:T(8,128)}, f32[512,8,8,8]{0,3,2,1:T(8,128)}, f32[512,8,8,8]{0,3,2,1:T(8,128)S(1)}) fusion(f32[512,9,9,9]{0,3,2,1:T(8,128)S(1)} %fusion.14, f32[512,8,8,8]{0,3,2,1:T(8,128)S(1)} %reshape.795), kind=kLoop, calls=%fused_computation.35 | loop fusion | flops 1048576 | bytes 9437184 | tf_op jit(solution)/shard_map/while/body/eval_jaxpr/sub | solution.py:67
  111.3 1.3 copy.105
  112.7 2.2 %maximum_bitcast_fusion = f32[512,3,512]{0,2,1:T(8,128)S(1)} fusion(f32[512,1,1,512]{0,3,2,1:T(8,128)} %bitcast.113, f32[512,1,1,512]{0,3,2,1:T(8,128)} %bitcast.114, f32[512,1,1,512]{0,3,2,1:T(8,128)} %bitcast.112), kind=kLoop, calls=%fused_computation.13 | loop fusion | flops 1572864 | bytes 6291456 | tf_op jit(solution)/shard_map/while/body/eval_jaxpr/mul | solution.py:70
  114.8 3.5 %copy.78 = f32[512,3,512]{2,1,0:T(4,128)} copy(f32[512,3,512]{0,2,1:T(8,128)S(1)} %maximum_bitcast_fusion) | data formatting | bytes 6291456 | tf_op jit(solution)/shard_map/while/body/eval_jaxpr/mul | solution.py:70
  118.3 31.3 %fusion = f32[512,24,24]{2,1,0:T(8,128)} fusion(f32[24,512]{1,0:T(8,128)S(1)} %broadcast_bitcast_fusion, f32[512,3,512]{2,1,0:T(4,128)} %copy.78), kind=kOutput, calls=%fused_computation.4 | convolution fusion | flops 1818230784 | bytes 4374528 | tf_op jit(solution)/shard_map/while/body/eval_jaxpr/hqy,hjy->hqj/dot_general | solution.py:72
  149.6 7.5 %fusion.3 = f32[512,24]{1,0:T(8,128)S(1)} fusion(f32[512,512]{1,0:T(8,128)S(1)} %copy-done.1, f32[24,512]{1,0:T(8,128)S(1)} %broadcast_bitcast_fusion, f32[512,3,512]{2,1,0:T(4,128)S(1)} %copy-done), kind=kLoop, calls=%fused_computation.7 | loop fusion | flops 18862080 | bytes 4292608
  157.1 0.1 copy.97
  157.3 4.4 %copy.80 = f32[512,24,24]{0,2,1:T(8,128)S(1)} copy(f32[512,24,24]{2,1,0:T(8,128)} %fusion) | data formatting | bytes 2359296 | tf_op jit(solution)/shard_map/while/body/eval_jaxpr/hqy,hjy->hqj/dot_general | solution.py:72
  161.7 0.1 broadcast_multiply_fusion
  161.8 0.8 copy.107
  162.6 0.7 gather_fusion.2
  163.5 0.1 pad_add_fusion
  163.6 3.1 %collective-permute-start = (f32[9,5,128]{2,1,0:T(8,128)S(1)}, f32[9,5,128]{2,1,0:T(8,128)S(1)}, u32[]{:S(2)}, u32[]{:S(2)}) collective-permute-start(f32[9,5,128]{2,1,0:T(8,128)S(1)} %slice_bitcast_fusion), channel_id=1, source_target_pairs={{0,1},{1,2},{2,3},{3,4},{4,5},{5,6},{6,7},{7,8},{8,9},{9,10},{10,1... | collective-permute-start | bytes 69128 | tf_op jit(solution)/shard_map/ppermute | solution.py:12
  166.7 6.2 %collective-permute-done = f32[9,5,128]{2,1,0:T(8,128)S(1)} collective-permute-done((f32[9,5,128]{2,1,0:T(8,128)S(1)}, f32[9,5,128]{2,1,0:T(8,128)S(1)}, u32[]{:S(2)}, u32[]{:S(2)}) %collective-permute-start) | collective-permute-done | bytes 23072 | tf_op jit(solution)/shard_map/ppermute | solution.py:12
  173.0 1.3 collective-permute-start.1
  174.3 0.4 reshape.794
  174.7 1.1 copy.92
  175.8 0.3 collective-permute-done.1
  176.1 0.6 copy-done.4
  (41 shorter events, 0.6 us)
Async XLA Ops:
  4.3 19.0 %all-to-all-start = ((s32[128,1,16]{2,1,0:T(1,128)}), s32[128,1,16]{2,1,0:T(1,128)S(1)}, u32[]{:S(2)}, u32[]{:S(2)}) async-start(s32[128,1,16]{2,1,0:T(1,128)} %bitcast.4), calls=%async_computation | async-start | bytes 131072 | tf_op jit(solution)/shard_map/all_to_all | solution.py:119
  38.2 6.7 %copy-start.2 = (bf16[1,1,4,1,128,512]{5,4,3,2,1,0:T(8,128)(2,1)S(1)}, bf16[1,1,4,1,128,512]{5,4,3,2,1,0:T(8,128)(2,1)}, u32[]{:S(2)}) copy-start(bf16[1,1,4,1,128,512]{5,4,3,2,1,0:T(8,128)(2,1)} %param.9) | copy-start | bytes 1572868
  38.3 58.8 %all-to-all-start.1 = ((bf16[128,16,1000]{2,1,0:T(8,128)(2,1)}), bf16[128,16,1000]{2,1,0:T(8,128)(2,1)}, u32[]{:S(2)}, u32[]{:S(2)}) async-start(bf16[128,16,1000]{2,1,0:T(8,128)(2,1)} %broadcast_select_fusion), calls=%async_computation.1 | async-start | bytes 8388608 | tf_op jit(solution)/shard_map/all_to_all | solution.py:124
  44.9 1.7 copy-start.3
  44.9 1.8 copy-start.5
  118.3 31.3 %copy-start = (f32[512,3,512]{2,1,0:T(4,128)S(1)}, f32[512,3,512]{2,1,0:T(4,128)}, u32[]{:S(2)}) copy-start(f32[512,3,512]{2,1,0:T(4,128)} %copy.78) | copy-start | bytes 9437188
  118.3 31.3 %copy-start.1 = (f32[512,512]{1,0:T(8,128)S(1)}, f32[512,512]{1,0:T(8,128)}, u32[]{:S(2)}) copy-start(f32[512,512]{1,0:T(8,128)} %copy.105) | copy-start | bytes 3145732
  163.6 9.3 %collective-permute-start = (f32[9,5,128]{2,1,0:T(8,128)S(1)}, f32[9,5,128]{2,1,0:T(8,128)S(1)}, u32[]{:S(2)}, u32[]{:S(2)}) collective-permute-start(f32[9,5,128]{2,1,0:T(8,128)S(1)} %slice_bitcast_fusion), channel_id=1, source_target_pairs={{0,1},{1,2},{2,3},{3,4},{4,5},{5,6},{6,7},{7,8},{8,9},{9,10},{10,1... | collective-permute-start | bytes 69128 | tf_op jit(solution)/shard_map/ppermute | solution.py:12
  173.0 3.1 %collective-permute-start.1 = (f32[9,1,128]{2,1,0:T(1,128)S(1)}, f32[9,1,128]{2,1,0:T(1,128)S(1)}, u32[]{:S(2)}, u32[]{:S(2)}) collective-permute-start(f32[9,1,128]{2,1,0:T(1,128)S(1)} %slice_bitcast_fusion.9), channel_id=1, source_target_pairs={{0,64},{1,65},{2,66},{3,67},{4,68},{5,69},{6,70},{7,71},{8,72},{9,... | collective-permute-start | bytes 13832 | tf_op jit(solution)/shard_map/ppermute | solution.py:12
  176.1 0.6 copy-start.4
where the time goes:
time: 179 us; the launch traced here: 177 us
  waiting for transfers between devices  63.5 us (35%)
  local copies, waits for them, and re-layouts  36 us (20%)
  matrix products  31.3 us (17%)
  other arithmetic  23.1 us (13%)
  starting transfers between devices  21.8 us (12%)
    all_to_all x1, waiting for transfers between devices, per_device(): lax.all_to_all(rows.reshape(lead + (rows.shape[-1],)), ('gz', 'xy'), spli...  50.3 us
    dot_general x1, matrix products, element_terms(): jnp.einsum('hqy,hjy->hqj', jacobian_matrix, jacobian_matrix, precision=la...  31.3 us
    all_to_all x1, starting transfers between devices, per_device(): lax.all_to_all(want_ids, ('gz', 'xy'), split_axis=0, concat_axis=0, tiled...  10.8 us
    gather x1, local copies, waits for them, and re-layouts, per_device(): rows = jnp.take(local_bricks, req_ids.reshape(-1), axis=0)  9.69 us
    gather x3, local copies, waits for them, and re-layouts, per_device(): rows = jnp.take(received_bricks, target, axis=0)  8.92 us
    unnamed x1, other arithmetic  7.52 us
    all_to_all x1, waiting for transfers between devices, per_device(): lax.all_to_all(want_ids, ('gz', 'xy'), split_axis=0, concat_axis=0, tiled...  6.68 us
    all_to_all x1, starting transfers between devices, per_device(): lax.all_to_all(rows.reshape(lead + (rows.shape[-1],)), ('gz', 'xy'), spli...  6.67 us
  transfers between devices with their start and end apart: 4, of which 4 were waited for; matrix products, arithmetic and copies ran while one was open for 3% of the time, Pallas kernels for 0%

commit v1 on v0

v1 whole, which is shorter than its diff:
```python
import functools

import jax
import jax.numpy as jnp
import ml_dtypes
import numpy as np
from jax import lax
from jax.experimental import pallas as pl
from jax.experimental.pallas import tpu as pltpu
from jax.sharding import PartitionSpec as P

MESH = pl.DeviceIdType.MESH
CAP = 16
BF = jnp.bfloat16
F32 = jnp.float32
NT = (((1,), (1,)), ((), ()))


def bf16_const(values):
    return np.asarray(values, np.float32).astype(ml_dtypes.bfloat16)


def selection_table():
    where = [(j, k) for j in range(8) for k in range(8)]
    where += [(j, 8) for j in range(8)] + [(8, k) for k in range(8)]
    table = np.zeros((4, 320, 112), np.float32)
    for phase in range(4):
        for shift in range(4):
            for row, (j, k) in enumerate(where):
                src = (j + shift // 2) * 10 + k + shift % 2
                table[phase, shift * 80 + row, phase * 4 + src] = 1.0
    return bf16_const(table)


def slope_table():
    def at(i, j, k):
        if i == 8:
            return 640 + j * 8 + k
        if k == 8:
            return 512 + i * 16 + j
        if j == 8:
            return 512 + i * 16 + 8 + k
        return i * 64 + j * 8 + k

    table = np.zeros((768, 1536), np.float32)
    for i in range(8):
        for j in range(8):
            for k in range(8):
                v = at(i, j, k)
                for c, up in enumerate((at(i + 1, j, k), at(i, j + 1, k), at(i, j, k + 1))):
                    table[up, c * 512 + v] = 1.0
                    table[v, c * 512 + v] = -1.0
    return bf16_const(table)


def split_rows(rows):
    high = bf16_const(rows)
    low = bf16_const(rows - high.astype(np.float64))
    return np.concatenate([high, low], axis=0)


def shape_tables():
    t = (np.arange(8, dtype=np.float64) + 0.5) / 8.0
    rows = []
    for n in range(8):
        az = t if n // 4 else 1.0 - t
        ax = t if n // 2 % 2 else 1.0 - t
        ay = t if n % 2 else 1.0 - t
        rows.append((az[:, None, None] * ax[None, :, None] * ay[None, None, :]).reshape(512))
    shape = np.stack(rows)
    full = (shape[:, None, :] * shape[None, :, :]).reshape(64, 512) / 64.0
    square = shape * shape / 64.0
    gram_rows = np.concatenate([split_rows(full), split_rows(square)], axis=0)
    return gram_rows, split_rows(shape / 64.0)


def exchange_kernel(
    own_ref, idx_ref, cls_ref, brick_ref, sel_ref, out_ref,
    t0, t1, merged, t2, tgt, lhs, wide, send, recv, acc,
    s1, r1, s2, r2, ss, rs,
):
    a = lax.axis_index("gz")
    b = lax.axis_index("xy")
    y, z, x = lax.div(b, 16), lax.rem(lax.div(b, 4), 4), lax.rem(b, 4)
    core = [a, 1 - a]
    x_up = [lax.rem(x + d, 4) for d in range(4)]
    y_up = [lax.rem(y + d, 4) for d in range(4)]
    z_up = [lax.rem(z + d, 4) for d in range(4)]
    line = [(core[p // 4], y * 16 + z * 4 + x_up[p % 4]) for p in range(8)]
    plane = [(a, y_up[q // 4] * 16 + z_up[q % 4] * 4 + x) for q in range(16)]

    barrier = pltpu.get_barrier_semaphore()
    for peer in line[1:] + plane[1:]:
        pl.semaphore_signal(barrier, inc=1, device_id=peer, device_id_type=MESH)

    def row_of(ref):
        return jnp.concatenate([ref[i] for i in range(4)], axis=1)

    owner, wanted, classes = row_of(own_ref), row_of(idx_ref), row_of(cls_ref)
    off_core = ((owner >> 6) + a) & 1
    off_y = ((owner >> 4) - y) & 3
    off_z = ((owner >> 2) - z) & 3
    off_x = (owner - x) & 3
    p_of = off_core * 4 + off_x
    q_of = off_y * 4 + off_z
    sub = lax.broadcasted_iota(jnp.int32, (128, 512), 0)
    hit = sub == p_of * 16 + q_of
    onehot = hit.astype(F32).astype(BF)
    before = (
        lax.broadcasted_iota(jnp.int32, (512, 512), 0)
        < lax.broadcasted_iota(jnp.int32, (512, 512), 1)
    ).astype(F32).astype(BF)
    ahead = jnp.dot(onehot, before, preferred_element_type=F32)
    slot = jnp.sum(jnp.where(hit, ahead, 0.0), axis=0, keepdims=True).astype(jnp.int32)
    target = (q_of * 8 + p_of) * CAP + slot
    tgt[...] = jnp.broadcast_to(target, (128, 512)).T
    in_slot = (sub & 15) == slot
    low = jnp.where(in_slot, wanted & 255, 0).astype(F32).astype(BF)
    high = jnp.where(in_slot, (wanted >> 8) + 2 * classes, 0).astype(F32).astype(BF)
    table = lax.dot_general(
        onehot, jnp.concatenate([low, high], axis=0), NT, preferred_element_type=F32
    )
    table = (table[:, :128] + 256.0 * table[:, 128:]).astype(jnp.int32)
    group = lax.broadcasted_iota(jnp.int32, (128, 128), 0) >> 4
    lane = lax.broadcasted_iota(jnp.int32, (128, 128), 1)
    t0[...] = jnp.where((lane >> 4) == group, table, 0).reshape(8, 16, 128)

    pl.semaphore_wait(barrier, 22)
    first = []
    for p in range(1, 8):
        copy = pltpu.make_async_remote_copy(
            t0.at[p], t1.at[p], s1.at[p], r1.at[p], device_id=line[p], device_id_type=MESH
        )
        copy.start()
        first.append(copy)
    t1[0] = t0[0]

    for i in range(10):
        start = 100 * i // 16 * 16
        depth = min(112, 1000 - start)
        window = jnp.concatenate([brick_ref[e, start : start + depth, :] for e in range(4)], axis=1)
        picked = jnp.dot(
            sel_ref[100 * i % 16 // 4, :, :depth], window, preferred_element_type=F32
        ).astype(BF)
        for shift in range(4):
            lhs[i * 80 : i * 80 + 80, shift * 512 : shift * 512 + 512] = picked[
                shift * 80 : shift * 80 + 80
            ]
    wide[704:768, :] = jnp.zeros((64, 128), BF)

    for copy in first:
        copy.wait()
    rows = jnp.sum(t1[...], axis=0)
    for q in range(16):
        merged[q] = rows[q : q + 1]
    t2[0] = rows[0:1]

    def second(q):
        return pltpu.make_async_remote_copy(
            merged.at[q], t2.at[q], s2.at[q], r2.at[q], device_id=plane[q], device_id_type=MESH
        )

    for q in range(1, 16):
        second(q).start()

    element = lax.broadcasted_iota(jnp.int32, (512, 128), 0)
    eye = (
        lax.broadcasted_iota(jnp.int32, (128, 128), 0)
        == lax.broadcasted_iota(jnp.int32, (128, 128), 1)
    ).astype(F32).astype(BF)
    x_down = [lax.rem(x + 4 - d, 4) for d in range(4)]

    def serve(step, carry):
        @pl.when(step == 1)
        def _():
            for q in range(1, 16):
                second(q).wait()

        q = lax.rem(step * 5, 16)
        request = t2[q]
        brick = request & 511
        cls = request >> 9
        fz = ((cls >> 4).astype(F32) + 0.5) * 0.25
        fx = (((cls >> 2) & 3).astype(F32) + 0.5) * 0.25
        fy = ((cls & 3).astype(F32) + 0.5) * 0.25
        match = element == brick
        weights = []
        for shift in range(4):
            wx = fx if shift // 2 else 1.0 - fx
            wy = fy if shift % 2 else 1.0 - fy
            weights.append(jnp.where(match, wx * wy, 0.0).astype(BF))
        layers = jnp.dot(lhs[...], jnp.concatenate(weights, axis=0), preferred_element_type=F32)
        for i in range(9):
            here = layers[i * 80 : i * 80 + 80] * (1.0 - fz)
            here = here + (layers[i * 80 + 80 : i * 80 + 160] * fz)
            here = here.astype(BF)
            if i < 8:
                wide[i * 64 : i * 64 + 64, :] = here[:64]
                wide[512 + i * 16 : 528 + i * 16, :] = here[64:]
            else:
                wide[640:704, :] = here[:64]
        send[q] = lax.dot_general(eye, wide[...], NT, preferred_element_type=F32).astype(BF)
        yy = lax.rem(y + 4 - lax.div(q, 4), 4)
        zz = lax.rem(z + 4 - lax.rem(q, 4), 4)
        for p in range(8):
            def go(p=p):
                pltpu.make_async_remote_copy(
                    send.at[q, pl.ds(p * CAP, CAP)],
                    recv.at[q, pl.ds(p * CAP, CAP)],
                    ss.at[q],
                    rs.at[q],
                    device_id=(core[p // 4], yy * 16 + zz * 4 + x_down[p % 4]),
                    device_id_type=MESH,
                ).start()

            if p == 0:
                pl.when(step > 0)(go)
            else:
                go()
        return carry

    lax.fori_loop(0, 16, serve, 0)
    recv[0, :CAP, :] = send[0, :CAP, :]
    acc[...] = jnp.zeros_like(acc)
    lanes = lax.broadcasted_iota(jnp.int32, (512, 128), 1)

    def whole(q, lo):
        part = pl.ds(lo, 128 - lo)
        return pltpu.make_async_remote_copy(
            send.at[q, part], recv.at[q, part], ss.at[q], rs.at[q],
            device_id=line[1], device_id_type=MESH,
        )

    def place(step, carry):
        q = lax.rem(step * 5, 16)

        @pl.when(step == 0)
        def _():
            whole(0, CAP).wait_recv()

        @pl.when(step > 0)
        def _():
            whole(q, 0).wait_recv()

        pick = jnp.where(tgt[...] == lanes + q * 128, 1.0, 0.0).astype(BF)
        acc[...] += jnp.dot(pick, recv[q], preferred_element_type=F32)
        return carry

    lax.fori_loop(0, 16, place, 0)
    out_ref[...] = acc[...].astype(BF)
    whole(0, CAP).wait_send()
    for q in range(1, 16):
        whole(q, 0).wait_send()


def exchange(owner, wanted, classes, bricks):
    vmem = pl.BlockSpec(memory_space=pltpu.VMEM)
    dma = pltpu.SemaphoreType.DMA
    return pl.pallas_call(
        exchange_kernel,
        out_shape=jax.ShapeDtypeStruct((512, 768), BF),
        in_specs=[vmem] * 5,
        out_specs=vmem,
        scratch_shapes=[
            pltpu.VMEM((8, 16, 128), jnp.int32),
            pltpu.VMEM((8, 16, 128), jnp.int32),
            pltpu.VMEM((16, 1, 128), jnp.int32),
            pltpu.VMEM((16, 1, 128), jnp.int32),
            pltpu.VMEM((512, 128), jnp.int32),
            pltpu.VMEM((800, 2048), BF),
            pltpu.VMEM((768, 128), BF),
            pltpu.VMEM((16, 128, 768), BF),
            pltpu.VMEM((16, 128, 768), BF),
            pltpu.VMEM((512, 768), F32),
            dma((8,)),
            dma((8,)),
            dma((16,)),
            dma((16,)),
            dma((16,)),
            dma((16,)),
        ],
        compiler_params=pltpu.CompilerParams(
            collective_id=0, has_side_effects=True, vmem_limit_bytes=40 << 20
        ),
    )(owner, wanted, classes, bricks, jnp.asarray(selection_table()))


PAIRS = ((0, 0), (0, 1), (0, 2), (1, 1), (1, 2), (2, 2))


def assemble_kernel(w_ref, img_ref, slope_ref, gram_tab, force_tab, gram_ref, own_ref, face_ref):
    lane = lax.broadcasted_iota(jnp.int32, (8, 128), 1)
    own = [None] * 5
    face = [None] * 5

    def add(old, new):
        return new if old is None else [u + v for u, v in zip(old, new)]

    for e in range(4):
        w = w_ref[e * 128 : e * 128 + 128, :]
        g = jnp.dot(w, slope_ref[...], preferred_element_type=F32)
        g = [g[:, c * 512 : c * 512 + 512] for c in range(3)]
        r = w[:, :512].astype(F32) - img_ref[e * 128 : e * 128 + 128, :].astype(F32)
        products = jnp.concatenate([(g[c] * g[d]).astype(BF) for c, d in PAIRS], axis=0)
        forces = jnp.concatenate([(g[c] * r).astype(BF) for c in range(3)], axis=0)
        sums = lax.dot_general(gram_tab[...], products, NT, preferred_element_type=F32)
        full = sums[:64] + sums[64:128]
        square = sums[128:136] + sums[136:144]
        force = lax.dot_general(force_tab[...], forces, NT, preferred_element_type=F32)
        force = force[:8] + force[8:]
        for c in range(3):
            for d in range(3):
                at = PAIRS.index((min(c, d), max(c, d))) * 128
                for n in range(8):
                    row = (c * 8 + n) * 24 + d * 8
                    gram_ref[e, row : row + 8, :] = full[n * 8 : n * 8 + 8, at : at + 128]
        terms = [force[:, c * 128 : c * 128 + 128] for c in range(3)]
        terms += [square[:, c * 128 : c * 128 + 128] for c in range(6)]
        both = []
        for t in terms:
            moved = jnp.where(lane == 0, 0.0, pltpu.roll(t, 1, 1))
            both.append(t + pltpu.roll(moved, 7, 0))
        own[e] = add(own[e], [t[0:1] for t in both])
        face[e] = add(face[e], [t[2:3] for t in both])
        own[e + 1] = [t[4:5] for t in both]
        face[e + 1] = [t[6:7] for t in both]
    for e in range(5):
        for c in range(9):
            own_ref[c, e : e + 1, :] = own[e][c]
            face_ref[c, e : e + 1, :] = face[e][c]


def assemble(samples, image):
    vmem = pl.BlockSpec(memory_space=pltpu.VMEM)
    gram_rows, force_rows = shape_tables()
    return pl.pallas_call(
        assemble_kernel,
        out_shape=(
            jax.ShapeDtypeStruct((4, 576, 128), F32),
            jax.ShapeDtypeStruct((9, 5, 128), F32),
            jax.ShapeDtypeStruct((9, 5, 128), F32),
        ),
        in_specs=[vmem] * 5,
        out_specs=(vmem,) * 3,
        compiler_params=pltpu.CompilerParams(vmem_limit_bytes=40 << 20),
    )(
        samples,
        image,
        jnp.asarray(slope_table()),
        jnp.asarray(gram_rows),
        jnp.asarray(force_rows),
    )


def passed_along(x, axis):
    size = lax.axis_size(axis)
    return lax.ppermute(x, axis, [(i, i + 1) for i in range(size - 1)])


def per_device(image, bricks, owner, brick_index, offset_class):
    bricks = jnp.transpose(bricks.reshape(4, 128, 1000), (0, 2, 1))
    samples = exchange(
        owner.reshape(4, 1, 128),
        brick_index.reshape(4, 1, 128),
        offset_class.reshape(4, 1, 128),
        bricks,
    )
    gram, own, face = assemble(samples, image.reshape(512, 512))
    own = own + passed_along(face, "xy")
    lid = passed_along(own[:, 4, :], "gz")
    nodes = own[:, :4, :].at[:, 0, :].add(lid).reshape(9, 4, 1, 128)
    return (nodes, jnp.transpose(gram, (0, 2, 1)).reshape(1, 1, 4, 1, 128, 576))


def solution(mesh):
    wide = P("gz", "xy", None, None, None, None)
    narrow = P("gz", "xy", None, None, None)
    return jax.shard_map(
        per_device,
        mesh=mesh,
        in_specs=(wide, wide, wide, narrow, narrow),
        out_specs=(P(None, "gz", "xy", None), wide),
        check_vma=False,
    )
```

time: 179 us -> 84.5 us (0.47); the launches traced: 177 us -> 84.1 us
  Pallas kernels: 0 us -> 62.7 us
  waiting for transfers between devices: 63.5 us -> 8.99 us
  matrix products: 31.3 us -> 0 us
  local copies, waits for them, and re-layouts: 36 us -> 8.19 us
  other arithmetic: 23.1 us -> 0.01 us
  starting transfers between devices: 21.8 us -> 3.46 us
    pallas_call x0 -> x2, Pallas kernels: none -> 62.7 us  [the longest x1 58.7 us: exchange(): pl.pallas_call(exchange_kernel, out_shape=jax.ShapeDtypeStruct((512, 768)...]
    all_to_all x2 -> x0, waiting for transfers between devices: 57 us -> none  [the longest x1 50.3 us: per_device(): lax.all_to_all(rows.reshape(lead + (rows.shape[-1],)), ('gz', 'xy'), spli...]
    dot_general x1 -> x0, matrix products: 31.3 us -> none  [element_terms(): jnp.einsum('hqy,hjy->hqj', jacobian_matrix, jacobian_matrix, precision=la...]
    gather x5 -> x0, local copies, waits for them, and re-layouts: 19.3 us -> none  [the longest x1 9.69 us: per_device(): rows = jnp.take(local_bricks, req_ids.reshape(-1), axis=0)]
    all_to_all x2 -> x0, starting transfers between devices: 17.4 us -> none  [the longest x1 10.8 us: per_device(): lax.all_to_all(want_ids, ('gz', 'xy'), split_axis=0, concat_axis=0, tiled...]
    unnamed x1 -> x0, other arithmetic: 7.52 us -> none
    dot_general x2 -> x0, local copies, waits for them, and re-layouts: 4.45 us -> none  [the longest x1 4.36 us: element_terms(): jnp.einsum('hqy,hjy->hqj', jacobian_matrix, jacobian_matrix, precision=la...]
    mul x10 -> x0, local copies, waits for them, and re-layouts: 4.22 us -> none  [the longest x2 3.51 us: element_terms(): slopes * shape_table()[None, None, :, :]]
  transfers between devices with their start and end apart: 4 -> 2, of which waited for: 4 -> 2; matrix products, arithmetic and copies ran while one was open for 3% -> 0% of each run, Pallas kernels for 0% -> 0%
where the time goes in v1:
time: 84.5 us; the launch traced here: 84.1 us
  Pallas kernels  62.7 us (74%)
  waiting for transfers between devices  8.99 us (11%)
  local copies, waits for them, and re-layouts  8.19 us (10%)
  starting transfers between devices  3.46 us (4%)
    pallas_call x1, Pallas kernels, exchange(): pl.pallas_call(exchange_kernel, out_shape=jax.ShapeDtypeStruct((512, 768)...  58.7 us
    ppermute x2, waiting for transfers between devices, passed_along(): return lax.ppermute(x, axis, [(i, i + 1) for i in range(size - 1)])  8.99 us
    unnamed x21, local copies, waits for them, and re-layouts  8.12 us
    pallas_call x1, Pallas kernels, assemble(): pl.pallas_call(assemble_kernel, out_shape=(jax.ShapeDtypeStruct((4, 576,...  4.04 us
    ppermute x2, starting transfers between devices, passed_along(): return lax.ppermute(x, axis, [(i, i + 1) for i in range(size - 1)])  3.46 us
  transfers between devices with their start and end apart: 2, of which 2 were waited for; matrix products, arithmetic and copies ran while one was open for 0% of the time, Pallas kernels for 0%

profile of v1, /device:TPU:9, one launch (start us, length us, event | category | flops | bytes accessed | tf_op | source)
XLA Modules:
  0.0 84.1 jit_solution(14764075040672397438)
XLA Ops:
  0.6 0.0 copy-start.1
  0.6 1.2 %copy-done.1 = bf16[1,1,4,1,128,1000]{4,5,3,2,1,0:T(8,128)(2,1)S(1)} copy-done((bf16[1,1,4,1,128,1000]{4,5,3,2,1,0:T(8,128)(2,1)S(1)}, bf16[1,1,4,1,128,1000]{4,5,3,2,1,0:T(8,128)(2,1)}, u32[]{:S(2)}) %copy-start.1) | copy-done | bytes 1024024
  1.8 0.0 copy-start.3
  1.9 1.0 %copy-done.3 = bf16[4,320,112]{2,1,0:T(8,128)(2,1)S(1)} copy-done((bf16[4,320,112]{2,1,0:T(8,128)(2,1)S(1)}, bf16[4,320,112]{2,1,0:T(8,128)(2,1)}, u32[]{:S(2)}) %copy-start.3) | copy-done | bytes 286744
  2.8 0.0 copy-start.6
  2.8 0.7 copy-done.6
  3.5 0.0 copy-start.7
  3.5 0.7 copy-done.7
  4.2 0.0 copy-start.8
  4.2 0.7 copy-done.8
  4.9 0.0 copy-start.2
  4.9 58.7 %shard_map.104.w_ref = bf16[512,768]{1,0:T(8,128)(2,1)S(1)} custom-call(s32[4,1,128]{2,1,0:T(1,128)S(1)} %bitcast.24, s32[4,1,128]{2,1,0:T(1,128)S(1)} %bitcast.25, s32[4,1,128]{2,1,0:T(1,128)S(1)} %bitcast.26, bf16[4,1000,128]{2,1,0:T(8,128)(2,1)S(1)} %bitcast.22, bf16[4,320,112]{2,1,0:T(8,128)(2,1)S(1)} %copy-done.3), custom_call_target="tpu_custom_call" | custom-call | tf_op jit(solution)/shard_map/pallas_call | solution.py:259
  63.6 0.0 copy-done.2
  63.6 0.0 copy-start
  63.6 1.7 %copy-done = bf16[768,1536]{1,0:T(8,128)(2,1)S(1)} copy-done((bf16[768,1536]{1,0:T(8,128)(2,1)S(1)}, bf16[768,1536]{1,0:T(8,128)(2,1)}, u32[]{:S(2)}) %copy-start) | copy-done | bytes 2359320
  65.2 0.0 copy-start.4
  65.2 0.9 %copy-done.4 = bf16[144,512]{1,0:T(8,128)(2,1)S(1)} copy-done((bf16[144,512]{1,0:T(8,128)(2,1)S(1)}, bf16[144,512]{1,0:T(8,128)(2,1)}, u32[]{:S(2)}) %copy-start.4) | copy-done | bytes 147480
  66.2 0.0 copy-start.5
  66.2 0.7 copy-done.5
  66.9 4.0 %shard_map.105 = (f32[4,576,128]{2,1,0:T(8,128)}, f32[9,5,128]{2,1,0:T(8,128)S(1)}, f32[9,5,128]{2,1,0:T(8,128)S(1)}) custom-call(bf16[512,768]{1,0:T(8,128)(2,1)S(1)} %shard_map.104.w_ref, bf16[512,512]{1,0:T(8,128)(2,1)S(1)} %bitcast.23, bf16[768,1536]{1,0:T(8,128)(2,1)S(1)} %copy-done, bf16[144,512]{1,0:T(8,128)(2,1)S(1)} %copy-done.4, ...), custom_call_target="tpu_custom_call" | custom-call | tf_op jit(solution)/shard_map/pallas_call | solution.py:336
  70.9 2.2 %collective-permute-start = (f32[9,5,128]{2,1,0:T(8,128)S(1)}, f32[9,5,128]{2,1,0:T(8,128)S(1)}, u32[]{:S(2)}, u32[]{:S(2)}) collective-permute-start(f32[9,5,128]{2,1,0:T(8,128)S(1)} %get-tuple-element.18), channel_id=1, source_target_pairs={{0,1},{1,2},{2,3},{3,4},{4,5},{5,6},{6,7},{7,8},{8,9},{9,10},{10,1... | collective-permute-start | bytes 69128 | tf_op jit(solution)/shard_map/ppermute | solution.py:357
  73.1 6.7 %collective-permute-done = f32[9,5,128]{2,1,0:T(8,128)S(1)} collective-permute-done((f32[9,5,128]{2,1,0:T(8,128)S(1)}, f32[9,5,128]{2,1,0:T(8,128)S(1)}, u32[]{:S(2)}, u32[]{:S(2)}) %collective-permute-start) | collective-permute-done | bytes 23072 | tf_op jit(solution)/shard_map/ppermute | solution.py:357
  79.8 1.3 %collective-permute-start.1 = (f32[9,128]{1,0:T(8,128)S(1)}, f32[9,128]{1,0:T(8,128)S(1)}, u32[]{:S(2)}, u32[]{:S(2)}) collective-permute-start(f32[9,128]{1,0:T(8,128)S(1)} %bitcast.28), channel_id=1, source_target_pairs={{0,64},{1,65},{2,66},{3,67},{4,68},{5,69},{6,70},{7,71},{8,72},{9,... | collective-permute-start | bytes 13832 | tf_op jit(solution)/shard_map/ppermute | solution.py:357
  81.2 2.3 %collective-permute-done.1 = f32[9,128]{1,0:T(8,128)S(1)} collective-permute-done((f32[9,128]{1,0:T(8,128)S(1)}, f32[9,128]{1,0:T(8,128)S(1)}, u32[]{:S(2)}, u32[]{:S(2)}) %collective-permute-start.1) | collective-permute-done | bytes 4640 | tf_op jit(solution)/shard_map/ppermute | solution.py:357
  83.5 0.0 copy-start.9
  83.5 0.6 copy-done.9
  (7 shorter events, 0.1 us)
Async XLA Ops:
  0.6 1.2 %copy-start.1 = (bf16[1,1,4,1,128,1000]{4,5,3,2,1,0:T(8,128)(2,1)S(1)}, bf16[1,1,4,1,128,1000]{4,5,3,2,1,0:T(8,128)(2,1)}, u32[]{:S(2)}) copy-start(bf16[1,1,4,1,128,1000]{4,5,3,2,1,0:T(8,128)(2,1)} %param.12) | copy-start | bytes 3072004
  1.8 1.0 %copy-start.3 = (bf16[4,320,112]{2,1,0:T(8,128)(2,1)S(1)}, bf16[4,320,112]{2,1,0:T(8,128)(2,1)}, u32[]{:S(2)}) copy-start(bf16[4,320,112]{2,1,0:T(8,128)(2,1)} %constant.36.clone.sel_ref) | copy-start | bytes 860164
  2.8 0.7 copy-start.6
  3.5 0.7 copy-start.7
  4.2 0.7 copy-start.8
  4.9 58.7 %copy-start.2 = (bf16[1,1,4,1,128,512]{5,4,3,2,1,0:T(8,128)(2,1)S(1)}, bf16[1,1,4,1,128,512]{5,4,3,2,1,0:T(8,128)(2,1)}, u32[]{:S(2)}) copy-start(bf16[1,1,4,1,128,512]{5,4,3,2,1,0:T(8,128)(2,1)} %param.11) | copy-start | bytes 1572868
  63.6 1.7 %copy-start = (bf16[768,1536]{1,0:T(8,128)(2,1)S(1)}, bf16[768,1536]{1,0:T(8,128)(2,1)}, u32[]{:S(2)}) copy-start(bf16[768,1536]{1,0:T(8,128)(2,1)} %constant.37.clone.slope_ref) | copy-start | bytes 7077892
  65.2 0.9 %copy-start.4 = (bf16[144,512]{1,0:T(8,128)(2,1)S(1)}, bf16[144,512]{1,0:T(8,128)(2,1)}, u32[]{:S(2)}) copy-start(bf16[144,512]{1,0:T(8,128)(2,1)} %constant.38.clone.gram_tab) | copy-start | bytes 442372
  66.2 0.7 copy-start.5
  70.9 8.9 %collective-permute-start = (f32[9,5,128]{2,1,0:T(8,128)S(1)}, f32[9,5,128]{2,1,0:T(8,128)S(1)}, u32[]{:S(2)}, u32[]{:S(2)}) collective-permute-start(f32[9,5,128]{2,1,0:T(8,128)S(1)} %get-tuple-element.18), channel_id=1, source_target_pairs={{0,1},{1,2},{2,3},{3,4},{4,5},{5,6},{6,7},{7,8},{8,9},{9,10},{10,1... | collective-permute-start | bytes 69128 | tf_op jit(solution)/shard_map/ppermute | solution.py:357
  79.8 3.6 %collective-permute-start.1 = (f32[9,128]{1,0:T(8,128)S(1)}, f32[9,128]{1,0:T(8,128)S(1)}, u32[]{:S(2)}, u32[]{:S(2)}) collective-permute-start(f32[9,128]{1,0:T(8,128)S(1)} %bitcast.28), channel_id=1, source_target_pairs={{0,64},{1,65},{2,66},{3,67},{4,68},{5,69},{6,70},{7,71},{8,72},{9,... | collective-permute-start | bytes 13832 | tf_op jit(solution)/shard_map/ppermute | solution.py:357
  83.5 0.6 copy-start.9

commit v2 on v1

v2 whole, which is shorter than its diff:
```python
import jax
import jax.numpy as jnp
import ml_dtypes
import numpy as np
from jax import lax
from jax.experimental import pallas as pl
from jax.experimental.pallas import tpu as pltpu
from jax.sharding import PartitionSpec as P

MESH = pl.DeviceIdType.MESH
CAP = 16
BF = jnp.bfloat16
F32 = jnp.float32
NT = (((1,), (1,)), ((), ()))


def bf16_const(values):
    return np.asarray(values, np.float32).astype(ml_dtypes.bfloat16)


def selection_table():
    where = [(j, k) for j in range(8) for k in range(8)]
    where += [(j, 8) for j in range(8)] + [(8, k) for k in range(8)]
    table = np.zeros((4, 320, 128), np.float32)
    for phase in range(4):
        for shift in range(4):
            for row, (j, k) in enumerate(where):
                src = (j + shift // 2) * 10 + k + shift % 2
                table[phase, shift * 80 + row, phase * 4 + src] = 1.0
    return bf16_const(table)


def slope_table():
    def at(i, j, k):
        if i == 8:
            return 640 + j * 8 + k
        if k == 8:
            return 512 + i * 16 + j
        if j == 8:
            return 512 + i * 16 + 8 + k
        return i * 64 + j * 8 + k

    table = np.zeros((768, 1536), np.float32)
    for i in range(8):
        for j in range(8):
            for k in range(8):
                v = at(i, j, k)
                for c, up in enumerate((at(i + 1, j, k), at(i, j + 1, k), at(i, j, k + 1))):
                    table[up, c * 512 + v] = 1.0
                    table[v, c * 512 + v] = -1.0
    table[704:] = table[640:704]
    return bf16_const(table)


def split_rows(rows):
    high = bf16_const(rows)
    low = bf16_const(rows - high.astype(np.float64))
    return np.concatenate([high, low], axis=0)


def shape_tables():
    t = (np.arange(8, dtype=np.float64) + 0.5) / 8.0
    rows = []
    for n in range(8):
        az = t if n // 4 else 1.0 - t
        ax = t if n // 2 % 2 else 1.0 - t
        ay = t if n % 2 else 1.0 - t
        rows.append((az[:, None, None] * ax[None, :, None] * ay[None, None, :]).reshape(512))
    shape = np.stack(rows)
    full = (shape[:, None, :] * shape[None, :, :]).reshape(64, 512) / 64.0
    square = shape * shape / 64.0
    return np.concatenate([split_rows(full), split_rows(square), split_rows(shape / 64.0)], axis=0)


PAIRS = ((0, 0), (0, 1), (0, 2), (1, 1), (1, 2), (2, 2))
ROWS = 88


def kernel(
    own_hbm, idx_hbm, cls_hbm, brick_hbm, sel_hbm, img_hbm, slope_hbm, shape_hbm, nodes_ref, gram_ref,
    own_ref, idx_ref, cls_ref, brick_ref, sel_ref, img_ref, slope_ref, shape_ref, loaded,
    t0, t1, merged, t2, tgt, lhs, wide, send, recv, acc, full, part, face_in, lid_in, edge_in,
    s1, r1, s2, r2, ss, rs, hs, hr,
):
    a = lax.axis_index("gz")
    b = lax.axis_index("xy")
    y, z, x = lax.div(b, 16), lax.rem(lax.div(b, 4), 4), lax.rem(b, 4)
    core = [a, 1 - a]
    x_up = [lax.rem(x + d, 4) for d in range(4)]
    y_up = [lax.rem(y + d, 4) for d in range(4)]
    z_up = [lax.rem(z + d, 4) for d in range(4)]
    line = [(core[p // 4], y * 16 + z * 4 + x_up[p % 4]) for p in range(8)]
    plane = [(a, y_up[q // 4] * 16 + z_up[q % 4] * 4 + x) for q in range(16)]

    loads = []
    for n, (src, dst) in enumerate(
        (
            (own_hbm, own_ref),
            (idx_hbm, idx_ref),
            (cls_hbm, cls_ref),
            (brick_hbm, brick_ref),
            (sel_hbm, sel_ref),
            (img_hbm, img_ref),
            (slope_hbm, slope_ref),
            (shape_hbm, shape_ref),
        )
    ):
        loads.append(pltpu.make_async_copy(src, dst, loaded.at[n]))
        loads[-1].start()
    barrier = pltpu.get_barrier_semaphore()
    for peer in line[1:] + plane[1:]:
        pl.semaphore_signal(barrier, inc=1, device_id=peer, device_id_type=MESH)
    for n in range(3):
        loads[n].wait()

    def row_of(ref):
        return jnp.concatenate([ref[i] for i in range(4)], axis=1)

    owner, wanted, classes = row_of(own_ref), row_of(idx_ref), row_of(cls_ref)
    off_core = ((owner >> 6) + a) & 1
    off_y = ((owner >> 4) - y) & 3
    off_z = ((owner >> 2) - z) & 3
    off_x = (owner - x) & 3
    p_of = off_core * 4 + off_x
    q_of = off_y * 4 + off_z
    sub = lax.broadcasted_iota(jnp.int32, (128, 512), 0)
    hit = sub == p_of * 16 + q_of
    onehot = hit.astype(F32).astype(BF)
    before = (
        lax.broadcasted_iota(jnp.int32, (512, 512), 0)
        < lax.broadcasted_iota(jnp.int32, (512, 512), 1)
    ).astype(F32).astype(BF)
    ahead = jnp.dot(onehot, before, preferred_element_type=F32)
    slot = jnp.sum(jnp.where(hit, ahead, 0.0), axis=0, keepdims=True).astype(jnp.int32)
    target = (q_of * 8 + p_of) * CAP + slot
    tgt[...] = jnp.broadcast_to(target, (128, 512)).T
    in_slot = (sub & 15) == slot
    low = jnp.where(in_slot, wanted & 255, 0).astype(F32).astype(BF)
    high = jnp.where(in_slot, (wanted >> 8) + 2 * classes, 0).astype(F32).astype(BF)
    table = lax.dot_general(
        onehot, jnp.concatenate([low, high], axis=0), NT, preferred_element_type=F32
    )
    table = (table[:, :128] + 256.0 * table[:, 128:]).astype(jnp.int32)
    group = lax.broadcasted_iota(jnp.int32, (128, 128), 0) >> 4
    lane = lax.broadcasted_iota(jnp.int32, (128, 128), 1)
    t0[...] = jnp.where((lane >> 4) == group, table, 0).reshape(8, 16, 128)

    pl.semaphore_wait(barrier, 22)
    first = []
    for p in range(1, 8):
        copy = pltpu.make_async_remote_copy(
            t0.at[p], t1.at[p], s1.at[p], r1.at[p], device_id=line[p], device_id_type=MESH
        )
        copy.start()
        first.append(copy)
    t1[0] = t0[0]

    loads[3].wait()
    loads[4].wait()
    for i in range(10):
        start = 100 * i // 16 * 16
        depth = min(112, 1000 - start)
        window = jnp.concatenate([brick_ref[e, start : start + depth, :] for e in range(4)], axis=1)
        picked = jnp.dot(
            sel_ref[100 * i % 16 // 4, :, :depth], window, preferred_element_type=F32
        ).astype(BF)
        for shift in range(4):
            lhs[i * 80 : i * 80 + 80, shift * 512 : shift * 512 + 512] = picked[
                shift * 80 : shift * 80 + 80
            ]

    for copy in first:
        copy.wait()
    rows = jnp.sum(t1[...], axis=0)
    for q in range(16):
        merged[q] = rows[q : q + 1]
    t2[0] = rows[0:1]

    def second(q, to=line[1]):
        return pltpu.make_async_remote_copy(
            merged.at[q], t2.at[q], s2.at[q], r2.at[q], device_id=to, device_id_type=MESH
        )

    for q in range(1, 16):
        second(q, plane[q]).start()

    element = lax.broadcasted_iota(jnp.int32, (512, 128), 0)
    eye = (
        lax.broadcasted_iota(jnp.int32, (128, 128), 0)
        == lax.broadcasted_iota(jnp.int32, (128, 128), 1)
    ).astype(F32).astype(BF)
    x_down = [lax.rem(x + 4 - d, 4) for d in range(4)]

    def serve(step, carry):
        q = lax.rem(step * 5, 16)

        @pl.when(step > 0)
        def _():
            second(q).wait_recv()

        request = t2[q]
        brick = request & 511
        cls = request >> 9
        fz = ((cls >> 4).astype(F32) + 0.5) * 0.25
        fx = (((cls >> 2) & 3).astype(F32) + 0.5) * 0.25
        fy = ((cls & 3).astype(F32) + 0.5) * 0.25
        match = element == brick
        weights = []
        for shift in range(4):
            wx = fx if shift // 2 else 1.0 - fx
            wy = fy if shift % 2 else 1.0 - fy
            weights.append(jnp.where(match, wx * wy, 0.0).astype(BF))
        layers = jnp.dot(lhs[...], jnp.concatenate(weights, axis=0), preferred_element_type=F32)
        for i in range(9):
            here = layers[i * 80 : i * 80 + 80] * (1.0 - fz)
            here = here + (layers[i * 80 + 80 : i * 80 + 160] * fz)
            here = here.astype(BF)
            if i < 8:
                wide[i * 64 : i * 64 + 64, :] = here[:64]
                wide[512 + i * 16 : 528 + i * 16, :] = here[64:]
            else:
                wide[640:704, :] = here[:64]
                wide[704:768, :] = here[:64]
        rows = lax.dot_general(eye, wide[...], NT, preferred_element_type=F32)
        for p in range(8):
            top = p * CAP
            for t in range(5):
                send[q, p, t * CAP : t * CAP + CAP, :] = rows[
                    top : top + CAP, t * 128 : t * 128 + 128
                ].astype(BF)
            send[q, p, 80:ROWS, :] = jnp.where(
                half, rows[top : top + 8, 640:768], rows[top + 8 : top + 16, 640:768]
            ).astype(BF)
        yy = lax.rem(y + 4 - lax.div(q, 4), 4)
        zz = lax.rem(z + 4 - lax.rem(q, 4), 4)
        for p in range(8):

            def go(p=p):
                pltpu.make_async_remote_copy(
                    send.at[q, p],
                    recv.at[q, p],
                    ss.at[q],
                    rs.at[q],
                    device_id=(core[p // 4], yy * 16 + zz * 4 + x_down[p % 4]),
                    device_id_type=MESH,
                ).start()

            if p == 0:
                pl.when(step > 0)(go)
            else:
                go()
        return carry

    half = lax.broadcasted_iota(jnp.int32, (8, 128), 1) < 64
    lax.fori_loop(0, 16, serve, 0)
    recv[0, 0] = send[0, 0]
    acc[...] = jnp.zeros_like(acc)
    lanes = lax.broadcasted_iota(jnp.int32, (512, 128), 1)

    def whole(q, lo):
        group = pl.ds(lo, 8 - lo)
        return pltpu.make_async_remote_copy(
            send.at[q, group], recv.at[q, group], ss.at[q], rs.at[q],
            device_id=line[1], device_id_type=MESH,
        )

    def place(step, carry):
        q = lax.rem(step * 5, 16)

        @pl.when(step == 0)
        def _():
            whole(0, 1).wait_recv()

        @pl.when(step > 0)
        def _():
            whole(q, 0).wait_recv()

        pick = jnp.where(tgt[...] == lanes + q * 128, 1.0, 0.0).astype(BF)
        columns = [
            jnp.concatenate([recv[q, p, t * CAP : t * CAP + CAP, :] for p in range(8)], axis=0)
            for t in range(5)
        ]
        last = []
        for p in range(8):
            rest = recv[q, p, 80:ROWS, :].astype(F32)
            last += [jnp.where(half, rest, 0.0), jnp.where(half, 0.0, rest)]
        columns.append(jnp.concatenate(last, axis=0).astype(BF))
        acc[...] += jnp.dot(pick, jnp.concatenate(columns, axis=1), preferred_element_type=F32)
        return carry

    lax.fori_loop(0, 16, place, 0)

    for n in range(5, 8):
        loads[n].wait()
    lane = lax.broadcasted_iota(jnp.int32, (8, 128), 1)
    sums_of = [[None] * 5, [None] * 5]

    def add(old, new):
        return new if old is None else [u + v for u, v in zip(old, new)]

    for e in range(4):
        w = acc[e * 128 : e * 128 + 128, :].astype(BF)
        g = jnp.dot(w, slope_ref[...], preferred_element_type=F32)
        g = [g[:, c * 512 : c * 512 + 512] for c in range(3)]
        r = acc[e * 128 : e * 128 + 128, :512] - img_ref[e * 128 : e * 128 + 128, :].astype(F32)
        products = jnp.concatenate([(g[c] * g[d]).astype(BF) for c, d in PAIRS], axis=0)
        forces = jnp.concatenate([(g[c] * r).astype(BF) for c in range(3)], axis=0)
        sums = lax.dot_general(shape_ref[:144, :], products, NT, preferred_element_type=F32)
        full[e] = sums[:64] + sums[64:128]
        square = sums[128:136] + sums[136:144]
        force = lax.dot_general(shape_ref[144:160, :], forces, NT, preferred_element_type=F32)
        force = force[:8] + force[8:]
        terms = [force[:, c * 128 : c * 128 + 128] for c in range(3)]
        terms += [square[:, c * 128 : c * 128 + 128] for c in range(6)]
        both = []
        for t in terms:
            moved = jnp.where(lane == 0, 0.0, pltpu.roll(t, 1, 1))
            both.append(t + pltpu.roll(moved, 7, 0))
        for nx in range(2):
            sums_of[nx][e] = add(sums_of[nx][e], [t[2 * nx : 2 * nx + 1] for t in both])
            sums_of[nx][e + 1] = [t[4 + 2 * nx : 5 + 2 * nx] for t in both]
    part[...] = jnp.zeros_like(part)
    for nx in range(2):
        for e in range(5):
            for c in range(9):
                part[nx, e, c : c + 1, :] = sums_of[nx][e][c]

    right = lax.rem(b + 1, 64)
    to_face = pltpu.make_async_remote_copy(
        part.at[1, pl.ds(0, 4)], face_in, hs.at[0], hr.at[0], device_id=(a, right), device_id_type=MESH
    )
    to_lid = pltpu.make_async_remote_copy(
        part.at[0, 4], lid_in, hs.at[1], hr.at[1], device_id=(1 - a, b), device_id_type=MESH
    )
    to_edge = pltpu.make_async_remote_copy(
        part.at[1, 4], edge_in, hs.at[2], hr.at[2], device_id=(1 - a, right), device_id_type=MESH
    )
    pl.when(b < 63)(to_face.start)
    pl.when(a == 0)(to_lid.start)
    pl.when((a == 0) & (b < 63))(to_edge.start)
    for e in range(4):
        for c in range(3):
            for d in range(3):
                at = PAIRS.index((min(c, d), max(c, d))) * 128
                for n in range(8):
                    row = (c * 8 + n) * 24 + d * 8
                    gram_ref[e, row : row + 8, :] = full[e, n * 8 : n * 8 + 8, at : at + 128]

    @pl.when(b > 0)
    def _():
        to_face.wait_recv()
        part[0, :4] += face_in[...]

    @pl.when(a == 1)
    def _():
        to_lid.wait_recv()
        part[0, 0] += lid_in[...]

    @pl.when((a == 1) & (b > 0))
    def _():
        to_edge.wait_recv()
        part[0, 0] += edge_in[...]

    for e in range(4):
        for c in range(9):
            nodes_ref[c, e] = part[0, e, c : c + 1, :]
    pl.when(b < 63)(to_face.wait_send)
    pl.when(a == 0)(to_lid.wait_send)
    pl.when((a == 0) & (b < 63))(to_edge.wait_send)
    whole(0, 1).wait_send()
    for q in range(1, 16):
        second(q).wait_send()
        whole(q, 0).wait_send()


def run(owner, wanted, classes, bricks, image):
    vmem = pl.BlockSpec(memory_space=pltpu.VMEM)
    dma = pltpu.SemaphoreType.DMA
    ints = pltpu.VMEM((4, 1, 128), jnp.int32)
    return pl.pallas_call(
        kernel,
        out_shape=(
            jax.ShapeDtypeStruct((9, 4, 1, 128), F32),
            jax.ShapeDtypeStruct((4, 576, 128), F32),
        ),
        in_specs=[pl.BlockSpec(memory_space=pl.ANY)] * 8,
        out_specs=(vmem, vmem),
        scratch_shapes=[
            ints,
            ints,
            ints,
            pltpu.VMEM((4, 1000, 128), BF),
            pltpu.VMEM((4, 320, 128), BF),
            pltpu.VMEM((512, 512), BF),
            pltpu.VMEM((768, 1536), BF),
            pltpu.VMEM((160, 512), BF),
            dma((8,)),
            pltpu.VMEM((8, 16, 128), jnp.int32),
            pltpu.VMEM((8, 16, 128), jnp.int32),
            pltpu.VMEM((16, 1, 128), jnp.int32),
            pltpu.VMEM((16, 1, 128), jnp.int32),
            pltpu.VMEM((512, 128), jnp.int32),
            pltpu.VMEM((800, 2048), BF),
            pltpu.VMEM((768, 128), BF),
            pltpu.VMEM((16, 8, ROWS, 128), BF),
            pltpu.VMEM((16, 8, ROWS, 128), BF),
            pltpu.VMEM((512, 768), F32),
            pltpu.VMEM((4, 64, 768), F32),
            pltpu.VMEM((2, 5, 16, 128), F32),
            pltpu.VMEM((4, 16, 128), F32),
            pltpu.VMEM((16, 128), F32),
            pltpu.VMEM((16, 128), F32),
            dma((8,)),
            dma((8,)),
            dma((16,)),
            dma((16,)),
            dma((16,)),
            dma((16,)),
            dma((3,)),
            dma((3,)),
        ],
        compiler_params=pltpu.CompilerParams(
            collective_id=0, has_side_effects=True, vmem_limit_bytes=60 << 20
        ),
    )(
        owner,
        wanted,
        classes,
        bricks,
        jnp.asarray(selection_table()),
        image,
        jnp.asarray(slope_table()),
        jnp.asarray(shape_tables()),
    )


def per_device(image, bricks, owner, brick_index, offset_class):
    bricks = jnp.transpose(bricks.reshape(4, 128, 1000), (0, 2, 1))
    nodes, gram = run(
        owner.reshape(4, 1, 128),
        brick_index.reshape(4, 1, 128),
        offset_class.reshape(4, 1, 128),
        bricks,
        image.reshape(512, 512),
    )
    return (nodes, jnp.transpose(gram, (0, 2, 1)).reshape(1, 1, 4, 1, 128, 576))


def solution(mesh):
    wide = P("gz", "xy", None, None, None, None)
    narrow = P("gz", "xy", None, None, None)
    return jax.shard_map(
        per_device,
        mesh=mesh,
        in_specs=(wide, wide, wide, narrow, narrow),
        out_specs=(P(None, "gz", "xy", None), wide),
        check_vma=False,
    )
```

time: 84.5 us -> 67.4 us (0.80); the launches traced: 84.1 us -> 66.1 us
  waiting for transfers between devices: 8.99 us -> 0 us
  local copies, waits for them, and re-layouts: 8.19 us -> 3.69 us
  starting transfers between devices: 3.46 us -> 0 us
  Pallas kernels: 62.7 us -> 61.7 us
    ppermute x2 -> x0, waiting for transfers between devices: 8.99 us -> none  [passed_along(): return lax.ppermute(x, axis, [(i, i + 1) for i in range(size - 1)])]
    unnamed x21 -> x2, local copies, waits for them, and re-layouts: 8.12 us -> 3.69 us
    ppermute x2 -> x0, starting transfers between devices: 3.46 us -> none  [passed_along(): return lax.ppermute(x, axis, [(i, i + 1) for i in range(size - 1)])]
    pallas_call x2 -> x1, Pallas kernels: 62.7 us -> 61.7 us  [run(): pl.pallas_call(kernel, out_shape=(jax.ShapeDtypeStruct((9, 4, 1, 128), F3...]
  transfers between devices with their start and end apart: 2 -> 0, of which waited for: 2 -> 0; matrix products, arithmetic and copies ran while one was open for 0% -> 0% of each run, Pallas kernels for 0% -> 0%
where the time goes in v2:
time: 67.4 us; the launch traced here: 66.1 us
  Pallas kernels  61.7 us (92%)
  local copies, waits for them, and re-layouts  3.69 us (5%)
    pallas_call x1, Pallas kernels, run(): pl.pallas_call(kernel, out_shape=(jax.ShapeDtypeStruct((9, 4, 1, 128), F3...  61.7 us
    unnamed x2, local copies, waits for them, and re-layouts  3.69 us

profile of v2, /device:TPU:9, one launch (start us, length us, event | category | flops | bytes accessed | tf_op | source)
XLA Modules:
  0.0 66.1 jit_solution(16547073263088065220)
XLA Ops:
  0.6 61.7 %shard_map.95 = (f32[9,4,1,128]{3,2,1,0:T(1,128)}, f32[4,576,128]{2,1,0:T(8,128)}) custom-call(s32[4,1,128]{2,1,0:T(1,128)} %bitcast.15, s32[4,1,128]{2,1,0:T(1,128)} %bitcast.16, s32[4,1,128]{2,1,0:T(1,128)} %bitcast.17, bf16[4,1000,128]{2,1,0:T(8,128)(2,1)} %bitcast.13, bf16[4,320,128]{2,1,0:T(8,128)(2,1)} %constant.6.clone.sel_hbm, ...), custom_call_target="tpu_custom_call" | custom-call | tf_op jit(solution)/shard_map/pallas_call | solution.py:380
  62.4 1.3 %copy.13 = f32[9,4,1,128]{3,2,1,0:T(1,128)} copy(f32[9,4,1,128]{3,2,1,0:T(1,128)} %get-tuple-element.10) | data formatting | bytes 36864
  63.7 2.4 %copy.14 = f32[1,1,4,1,128,576]{4,5,3,2,1,0:T(8,128)} copy(f32[1,1,4,1,128,576]{4,5,3,2,1,0:T(8,128)} %bitcast.12) | data formatting | bytes 2359296

commit v3 on v2

--- a/solution.py
+++ b/solution.py
@@ -30,6 +30,9 @@
     return bf16_const(table)
 
 
+BLOCKS = ((0, 1), (1, 2), (0, 2), (1, 2), (0, 2), (1, 2))
+
+
 def slope_table():
     def at(i, j, k):
         if i == 8:
@@ -49,7 +52,13 @@
                     table[up, c * 512 + v] = 1.0
                     table[v, c * 512 + v] = -1.0
     table[704:] = table[640:704]
-    return bf16_const(table)
+    blocks = []
+    for n, (one, two) in enumerate(BLOCKS):
+        columns = table[:, n * 256 : n * 256 + 256]
+        blocks.append(
+            np.concatenate([columns[one * 256 : one * 256 + 256], columns[two * 256 : two * 256 + 256]])
+        )
+    return bf16_const(np.stack(blocks))
 
 
 def split_rows(rows):
@@ -73,14 +82,17 @@
 
 
 PAIRS = ((0, 0), (0, 1), (0, 2), (1, 1), (1, 2), (2, 2))
+LINE = 128
+LAG = 3
 ROWS = 88
 
 
 def kernel(
-    own_hbm, idx_hbm, cls_hbm, brick_hbm, sel_hbm, img_hbm, slope_hbm, shape_hbm, nodes_ref, gram_ref,
+    own_hbm, idx_hbm, cls_hbm, brick_hbm, sel_hbm, img_hbm, slope_hbm, shape_hbm, nodes_hbm, gram_hbm,
     own_ref, idx_ref, cls_ref, brick_ref, sel_ref, img_ref, slope_ref, shape_ref, loaded,
-    t0, t1, merged, t2, tgt, lhs, wide, send, recv, acc, full, part, face_in, lid_in, edge_in,
-    s1, r1, s2, r2, ss, rs, hs, hr,
+    t0, t1, merged, t2, tgt, lhs, wide, send_line, recv_line, send, recv, acc,
+    gram, nodes, part, face_in, lid_in, edge_in,
+    s1, r1, s2, r2, sl, rl, ss, rs, hs, hr, stored,
 ):
     a = lax.axis_index("gz")
     b = lax.axis_index("xy")
@@ -106,7 +118,8 @@
         )
     ):
         loads.append(pltpu.make_async_copy(src, dst, loaded.at[n]))
-        loads[-1].start()
+    for n in range(5):
+        loads[n].start()
     barrier = pltpu.get_barrier_semaphore()
     for peer in line[1:] + plane[1:]:
         pl.semaphore_signal(barrier, inc=1, device_id=peer, device_id_type=MESH)
@@ -132,7 +145,10 @@
     ).astype(F32).astype(BF)
     ahead = jnp.dot(onehot, before, preferred_element_type=F32)
     slot = jnp.sum(jnp.where(hit, ahead, 0.0), axis=0, keepdims=True).astype(jnp.int32)
-    target = (q_of * 8 + p_of) * CAP + slot
+    jy = (off_y - off_x) & 3
+    jz = (off_z - 2 * off_core - off_x) & 3
+    message = (jy * 2 + (jz >> 1)) * 16 + (jz & 1) * 8 + p_of
+    target = jnp.where(q_of == 0, LINE + p_of, message) * CAP + slot
     tgt[...] = jnp.broadcast_to(target, (128, 512)).T
     in_slot = (sub & 15) == slot
     low = jnp.where(in_slot, wanted & 255, 0).astype(F32).astype(BF)
@@ -154,6 +170,8 @@
         copy.start()
         first.append(copy)
     t1[0] = t0[0]
+    for n in range(5, 8):
+        loads[n].start()
 
     loads[3].wait()
     loads[4].wait()
@@ -169,8 +187,12 @@
                 shift * 80 : shift * 80 + 80
             ]
 
+    for p in range(8):
+        jy, jz = -(p % 4) % 4, (-2 * (p // 4) - p % 4) % 4
+        recv[jy * 2 + jz // 2, jz % 2 * 8 + p] = jnp.zeros((ROWS, 128), BF)
+    acc[...] = jnp.zeros_like(acc)
     for copy in first:
-        copy.wait()
+        copy.wait_recv()
     rows = jnp.sum(t1[...], axis=0)
     for q in range(16):
         merged[q] = rows[q : q + 1]
@@ -184,27 +206,22 @@
     for q in range(1, 16):
         second(q, plane[q]).start()
 
-    element = lax.broadcasted_iota(jnp.int32, (512, 128), 0)
     eye = (
-        lax.broadcasted_iota(jnp.int32, (128, 128), 0)
-        == lax.broadcasted_iota(jnp.int32, (128, 128), 1)
+        lax.broadcasted_iota(jnp.int32, (256, 256), 0)
+        == lax.broadcasted_iota(jnp.int32, (256, 256), 1)
     ).astype(F32).astype(BF)
+    half = lax.broadcasted_iota(jnp.int32, (8, 128), 1) < 64
+    slot_group = lax.broadcasted_iota(jnp.int32, (1, 128), 1) >> 4
     x_down = [lax.rem(x + 4 - d, 4) for d in range(4)]
 
-    def serve(step, carry):
-        q = lax.rem(step * 5, 16)
-
-        @pl.when(step > 0)
-        def _():
-            second(q).wait_recv()
-
-        request = t2[q]
+    def serve(request, out, post):
+        width = request.shape[1]
         brick = request & 511
         cls = request >> 9
         fz = ((cls >> 4).astype(F32) + 0.5) * 0.25
         fx = (((cls >> 2) & 3).astype(F32) + 0.5) * 0.25
         fy = ((cls & 3).astype(F32) + 0.5) * 0.25
-        match = element == brick
+        match = lax.broadcasted_iota(jnp.int32, (512, width), 0) == brick
         weights = []
         for shift in range(4):
             wx = fx if shift // 2 else 1.0 - fx
@@ -213,100 +230,162 @@
         layers = jnp.dot(lhs[...], jnp.concatenate(weights, axis=0), preferred_element_type=F32)
         for i in range(9):
             here = layers[i * 80 : i * 80 + 80] * (1.0 - fz)
-            here = here + (layers[i * 80 + 80 : i * 80 + 160] * fz)
+            here = here + layers[i * 80 + 80 : i * 80 + 160] * fz
             here = here.astype(BF)
             if i < 8:
-                wide[i * 64 : i * 64 + 64, :] = here[:64]
-                wide[512 + i * 16 : 528 + i * 16, :] = here[64:]
+                wide[i * 64 : i * 64 + 64, :width] = here[:64]
+                wide[512 + i * 16 : 528 + i * 16, :width] = here[64:]
             else:
-                wide[640:704, :] = here[:64]
-                wide[704:768, :] = here[:64]
-        rows = lax.dot_general(eye, wide[...], NT, preferred_element_type=F32)
-        for p in range(8):
-            top = p * CAP
+                wide[640:704, :width] = here[:64]
+                wide[704:768, :width] = here[:64]
+        rows = lax.dot_general(
+            eye[:width, :width], wide[:, :width], NT, preferred_element_type=F32
+        )
+        for m in range(width // CAP):
+            top = m * CAP
+            slab = out(m)
             for t in range(5):
-                send[q, p, t * CAP : t * CAP + CAP, :] = rows[
+                slab[t * CAP : t * CAP + CAP, :] = rows[
                     top : top + CAP, t * 128 : t * 128 + 128
                 ].astype(BF)
-            send[q, p, 80:ROWS, :] = jnp.where(
+            slab[80:ROWS, :] = jnp.where(
                 half, rows[top : top + 8, 640:768], rows[top + 8 : top + 16, 640:768]
             ).astype(BF)
-        yy = lax.rem(y + 4 - lax.div(q, 4), 4)
-        zz = lax.rem(z + 4 - lax.rem(q, 4), 4)
-        for p in range(8):
-
-            def go(p=p):
-                pltpu.make_async_remote_copy(
-                    send.at[q, p],
-                    recv.at[q, p],
-                    ss.at[q],
-                    rs.at[q],
-                    device_id=(core[p // 4], yy * 16 + zz * 4 + x_down[p % 4]),
-                    device_id_type=MESH,
-                ).start()
-
-            if p == 0:
-                pl.when(step > 0)(go)
-            else:
-                go()
-        return carry
-
-    half = lax.broadcasted_iota(jnp.int32, (8, 128), 1) < 64
-    lax.fori_loop(0, 16, serve, 0)
-    recv[0, 0] = send[0, 0]
-    acc[...] = jnp.zeros_like(acc)
-    lanes = lax.broadcasted_iota(jnp.int32, (512, 128), 1)
-
-    def whole(q, lo):
-        group = pl.ds(lo, 8 - lo)
-        return pltpu.make_async_remote_copy(
-            send.at[q, group], recv.at[q, group], ss.at[q], rs.at[q],
-            device_id=line[1], device_id_type=MESH,
-        )
-
-    def place(step, carry):
-        q = lax.rem(step * 5, 16)
-
-        @pl.when(step == 0)
-        def _():
-            whole(0, 1).wait_recv()
-
-        @pl.when(step > 0)
-        def _():
-            whole(q, 0).wait_recv()
-
-        pick = jnp.where(tgt[...] == lanes + q * 128, 1.0, 0.0).astype(BF)
+            post(m)
+
+    def samples_of(slabs):
         columns = [
-            jnp.concatenate([recv[q, p, t * CAP : t * CAP + CAP, :] for p in range(8)], axis=0)
+            jnp.concatenate([slab[t * CAP : t * CAP + CAP, :] for slab in slabs], axis=0)
             for t in range(5)
         ]
         last = []
-        for p in range(8):
-            rest = recv[q, p, 80:ROWS, :].astype(F32)
+        for slab in slabs:
+            rest = slab[80:ROWS, :].astype(F32)
             last += [jnp.where(half, rest, 0.0), jnp.where(half, 0.0, rest)]
         columns.append(jnp.concatenate(last, axis=0).astype(BF))
-        acc[...] += jnp.dot(pick, jnp.concatenate(columns, axis=1), preferred_element_type=F32)
+        return jnp.concatenate(columns, axis=1)
+
+    def pick_of(first, width):
+        lanes = lax.broadcasted_iota(jnp.int32, (512, 128), 1)
+        wanted_at = tgt[...]
+        return jnp.concatenate(
+            [
+                jnp.where(wanted_at == lanes + (first + 128 * n), 1.0, 0.0).astype(BF)
+                for n in range(width // 128)
+            ],
+            axis=1,
+        )
+
+    on_line = [
+        pltpu.make_async_remote_copy(
+            send_line.at[p],
+            recv_line.at[p],
+            sl.at[p],
+            rl.at[p],
+            device_id=(core[p // 4], y * 16 + z * 4 + x_down[p % 4]),
+            device_id_type=MESH,
+        )
+        for p in range(1, 8)
+    ]
+    serve(t2[0], lambda m: send_line.at[m], lambda m: on_line[m - 1].start() if m else None)
+    recv_line[0] = send_line[0]
+    for q in range(1, 16):
+        second(q).wait_recv()
+
+    def all_of(n):
+        return pltpu.make_async_remote_copy(
+            send.at[n, pl.ds(0, 15)], recv.at[n, pl.ds(0, 15)], ss.at[n], rs.at[n],
+            device_id=line[1], device_id_type=MESH,
+        )
+
+    def place(n):
+        all_of(n).wait_recv()
+        rows = jnp.concatenate(
+            [samples_of([recv.at[n, g * 8 + p] for p in range(8)]) for g in range(2)], axis=0
+        )
+        acc[...] += jnp.dot(pick_of(n * 256, 256), rows, preferred_element_type=F32)
+
+    def step(n, carry):
+        offsets = []
+        request = []
+        for g in range(2):
+            row = jnp.zeros((1, 128), jnp.int32)
+            for p in range(8):
+                dy = lax.rem(lax.div(n, 2) + p % 4, 4)
+                dz = lax.rem(2 * lax.rem(n, 2) + g + 2 * (p // 4) + p % 4, 4)
+                offsets.append((dy, dz))
+                row = jnp.where(slot_group == p, t2[dy * 4 + dz], row)
+            request.append(row)
+
+        def post(m):
+            dy, dz = offsets[m]
+
+            @pl.when(dy + dz > 0)
+            def _():
+                to = lax.rem(y + 4 - dy, 4) * 16 + lax.rem(z + 4 - dz, 4) * 4 + x_down[m % 4]
+                pltpu.make_async_remote_copy(
+                    send.at[n, m],
+                    recv.at[n, m],
+                    ss.at[n],
+                    rs.at[n],
+                    device_id=(core[m // 4 % 2], to),
+                    device_id_type=MESH,
+                ).start()
+
+        serve(jnp.concatenate(request, axis=1), lambda m: send.at[n, m], post)
+
+        @pl.when(n >= LAG)
+        def _():
+            place(n - LAG)
+
         return carry
 
-    lax.fori_loop(0, 16, place, 0)
+    lax.fori_loop(0, 8, step, 0)
+    for p in range(1, 8):
+        on_line[p - 1].wait_recv()
+    rows = samples_of([recv_line.at[p] for p in range(8)])
+    acc[...] += jnp.dot(pick_of(LINE * CAP, 128), rows, preferred_element_type=F32)
+
+    def rest(n, carry):
+        place(n)
+        return carry
+
+    lax.fori_loop(8 - LAG, 8, rest, 0)
 
     for n in range(5, 8):
         loads[n].wait()
     lane = lax.broadcasted_iota(jnp.int32, (8, 128), 1)
     sums_of = [[None] * 5, [None] * 5]
+    stores = []
 
     def add(old, new):
         return new if old is None else [u + v for u, v in zip(old, new)]
 
     for e in range(4):
         w = acc[e * 128 : e * 128 + 128, :].astype(BF)
-        g = jnp.dot(w, slope_ref[...], preferred_element_type=F32)
-        g = [g[:, c * 512 : c * 512 + 512] for c in range(3)]
+        blocks = [w[:, n * 256 : n * 256 + 256] for n in range(3)]
+        g = [
+            jnp.dot(
+                jnp.concatenate([blocks[one], blocks[two]], axis=1),
+                slope_ref[n],
+                preferred_element_type=F32,
+            )
+            for n, (one, two) in enumerate(BLOCKS)
+        ]
+        g = [jnp.concatenate(g[2 * c : 2 * c + 2], axis=1) for c in range(3)]
         r = acc[e * 128 : e * 128 + 128, :512] - img_ref[e * 128 : e * 128 + 128, :].astype(F32)
         products = jnp.concatenate([(g[c] * g[d]).astype(BF) for c, d in PAIRS], axis=0)
         forces = jnp.concatenate([(g[c] * r).astype(BF) for c in range(3)], axis=0)
         sums = lax.dot_general(shape_ref[:144, :], products, NT, preferred_element_type=F32)
-        full[e] = sums[:64] + sums[64:128]
+        full = sums[:64] + sums[64:128]
+        for c in range(3):
+            for d in range(3):
+                at = PAIRS.index((min(c, d), max(c, d))) * 128
+                for n in range(8):
+                    row = (c * 8 + n) * 24 + d * 8
+                    gram[e, row : row + 8, :] = full[n * 8 : n * 8 + 8, at : at + 128]
+        stores.append(pltpu.make_async_copy(gram.at[e], gram_hbm.at[e], stored.at[e]))
+        stores[-1].start()
         square = sums[128:136] + sums[136:144]
         force = lax.dot_general(shape_ref[144:160, :], forces, NT, preferred_element_type=F32)
         force = force[:8] + force[8:]
@@ -338,13 +417,6 @@
     pl.when(b < 63)(to_face.start)
     pl.when(a == 0)(to_lid.start)
     pl.when((a == 0) & (b < 63))(to_edge.start)
-    for e in range(4):
-        for c in range(3):
-            for d in range(3):
-                at = PAIRS.index((min(c, d), max(c, d))) * 128
-                for n in range(8):
-                    row = (c * 8 + n) * 24 + d * 8
-                    gram_ref[e, row : row + 8, :] = full[e, n * 8 : n * 8 + 8, at : at + 128]
 
     @pl.when(b > 0)
     def _():
@@ -363,28 +435,54 @@
 
     for e in range(4):
         for c in range(9):
-            nodes_ref[c, e] = part[0, e, c : c + 1, :]
+            nodes[c, e] = part[0, e, c : c + 1, :]
+    stores.append(pltpu.make_async_copy(nodes, nodes_hbm, stored.at[4]))
+    stores[-1].start()
     pl.when(b < 63)(to_face.wait_send)
     pl.when(a == 0)(to_lid.wait_send)
     pl.when((a == 0) & (b < 63))(to_edge.wait_send)
-    whole(0, 1).wait_send()
+    for p in range(1, 8):
+        first[p - 1].wait_send()
+        on_line[p - 1].wait_send()
     for q in range(1, 16):
         second(q).wait_send()
-        whole(q, 0).wait_send()
+    for n in range(8):
+        all_of(n).wait_send()
+    for store in stores:
+        store.wait()
+
+
+def copy_kernel(nodes_in, gram_in, nodes_out, gram_out, nodes, gram, came, went):
+    moves = [(gram_in.at[e], gram.at[e], gram_out.at[e]) for e in range(4)]
+    moves.append((nodes_in, nodes, nodes_out))
+    inward = [
+        pltpu.make_async_copy(src, mid, came.at[n]) for n, (src, mid, _) in enumerate(moves)
+    ]
+    outward = [
+        pltpu.make_async_copy(mid, dst, went.at[n]) for n, (_, mid, dst) in enumerate(moves)
+    ]
+    for copy in inward:
+        copy.start()
+    for before, after in zip(inward, outward):
+        before.wait()
+        after.start()
+    for copy in outward:
+        copy.wait()
 
 
 def run(owner, wanted, classes, bricks, image):
-    vmem = pl.BlockSpec(memory_space=pltpu.VMEM)
+    hbm = pl.BlockSpec(memory_space=pl.ANY)
     dma = pltpu.SemaphoreType.DMA
     ints = pltpu.VMEM((4, 1, 128), jnp.int32)
-    return pl.pallas_call(
+    outs = (
+        jax.ShapeDtypeStruct((9, 4, 1, 128), F32),
+        jax.ShapeDtypeStruct((4, 576, 128), F32),
+    )
+    made = pl.pallas_call(
         kernel,
-        out_shape=(
-            jax.ShapeDtypeStruct((9, 4, 1, 128), F32),
-            jax.ShapeDtypeStruct((4, 576, 128), F32),
-        ),
-        in_specs=[pl.BlockSpec(memory_space=pl.ANY)] * 8,
-        out_specs=(vmem, vmem),
+        out_shape=outs,
+        in_specs=[hbm] * 8,
+        out_specs=(hbm, hbm),
         scratch_shapes=[
             ints,
             ints,
@@ -392,7 +490,7 @@
             pltpu.VMEM((4, 1000, 128), BF),
             pltpu.VMEM((4, 320, 128), BF),
             pltpu.VMEM((512, 512), BF),
-            pltpu.VMEM((768, 1536), BF),
+            pltpu.VMEM((6, 512, 256), BF),
             pltpu.VMEM((160, 512), BF),
             dma((8,)),
             pltpu.VMEM((8, 16, 128), jnp.int32),
@@ -401,11 +499,14 @@
             pltpu.VMEM((16, 1, 128), jnp.int32),
             pltpu.VMEM((512, 128), jnp.int32),
             pltpu.VMEM((800, 2048), BF),
-            pltpu.VMEM((768, 128), BF),
-            pltpu.VMEM((16, 8, ROWS, 128), BF),
-            pltpu.VMEM((16, 8, ROWS, 128), BF),
+            pltpu.VMEM((768, 256), BF),
+            pltpu.VMEM((8, ROWS, 128), BF),
+            pltpu.VMEM((8, ROWS, 128), BF),
+            pltpu.VMEM((8, 16, ROWS, 128), BF),
+            pltpu.VMEM((8, 16, ROWS, 128), BF),
             pltpu.VMEM((512, 768), F32),
-            pltpu.VMEM((4, 64, 768), F32),
+            pltpu.VMEM((4, 576, 128), F32),
+            pltpu.VMEM((9, 4, 1, 128), F32),
             pltpu.VMEM((2, 5, 16, 128), F32),
             pltpu.VMEM((4, 16, 128), F32),
             pltpu.VMEM((16, 128), F32),
@@ -414,10 +515,13 @@
             dma((8,)),
             dma((16,)),
             dma((16,)),
-            dma((16,)),
-            dma((16,)),
+            dma((8,)),
+            dma((8,)),
+            dma((8,)),
+            dma((8,)),
             dma((3,)),
             dma((3,)),
+            dma((5,)),
         ],
         compiler_params=pltpu.CompilerParams(
             collective_id=0, has_side_effects=True, vmem_limit_bytes=60 << 20
@@ -432,6 +536,19 @@
         jnp.asarray(slope_table()),
         jnp.asarray(shape_tables()),
     )
+    return pl.pallas_call(
+        copy_kernel,
+        out_shape=outs,
+        in_specs=[hbm] * 2,
+        out_specs=(hbm, hbm),
+        scratch_shapes=[
+            pltpu.VMEM((9, 4, 1, 128), F32),
+            pltpu.VMEM((4, 576, 128), F32),
+            dma((5,)),
+            dma((5,)),
+        ],
+        compiler_params=pltpu.CompilerParams(vmem_limit_bytes=60 << 20),
+    )(*made)
 
 
 def per_device(image, bricks, owner, brick_index, offset_class):

time: 67.4 us -> 64.2 us (0.953); the launches traced: 66.1 us -> 64.1 us
  local copies, waits for them, and re-layouts: 3.69 us -> 0 us
  Pallas kernels: 61.7 us -> 63.4 us
    unnamed x2 -> x0, local copies, waits for them, and re-layouts: 3.69 us -> none
    pallas_call x1 -> x2, Pallas kernels: 61.7 us -> 63.4 us  [the longest x1 61.4 us: run(): pl.pallas_call(kernel, out_shape=outs, in_specs=[hbm] * 8, out_specs=(hbm...]
where the time goes in v3:
time: 64.2 us; the launch traced here: 64.1 us
  Pallas kernels  63.4 us (99%)
    pallas_call x1, Pallas kernels, run(): pl.pallas_call(kernel, out_shape=outs, in_specs=[hbm] * 8, out_specs=(hbm...  61.4 us
    pallas_call x1, Pallas kernels, run(): pl.pallas_call(copy_kernel, out_shape=outs, in_specs=[hbm] * 2, out_specs...  2.06 us

profile of v3, /device:TPU:9, one launch (start us, length us, event | category | flops | bytes accessed | tf_op | source)
XLA Modules:
  0.0 64.1 jit_solution(1708637689466833841)
XLA Ops:
  0.6 61.4 %shard_map.95 = (f32[9,4,1,128]{3,2,1,0:T(1,128)}, f32[4,576,128]{2,1,0:T(8,128)}) custom-call(s32[4,1,128]{2,1,0:T(1,128)} %bitcast.14, s32[4,1,128]{2,1,0:T(1,128)} %bitcast.15, s32[4,1,128]{2,1,0:T(1,128)} %bitcast.16, bf16[4,1000,128]{2,1,0:T(8,128)(2,1)} %bitcast.12, bf16[4,320,128]{2,1,0:T(8,128)(2,1)} %constant.6.clone.sel_hbm, ...), custom_call_target="tpu_custom_call" | custom-call | tf_op jit(solution)/shard_map/pallas_call | solution.py:481
  62.0 2.1 %shard_map.96 = (f32[9,4,1,128]{3,2,1,0:T(1,128)}, f32[4,576,128]{2,1,0:T(8,128)}) custom-call(f32[9,4,1,128]{3,2,1,0:T(1,128)} %get-tuple-element.6.nodes_in, f32[4,576,128]{2,1,0:T(8,128)} %get-tuple-element.7.gram_in), custom_call_target="tpu_custom_call" | custom-call | tf_op jit(solution)/shard_map/pallas_call | solution.py:539

commit v4 on v3

--- a/solution.py
+++ b/solution.py
@@ -82,17 +82,26 @@
 
 
 PAIRS = ((0, 0), (0, 1), (0, 2), (1, 1), (1, 2), (2, 2))
-LINE = 128
-LAG = 3
+LAG = 4
+FARTHEST_FIRST = sorted(
+    (
+        (-min(dy, 4 - dy) - min(dz, 4 - dz) - min(dx, 4 - dx), da, dy, dz, dx)
+        for da in range(2)
+        for dy in range(4)
+        for dz in range(4)
+        for dx in range(4)
+        if da or dy or dz or dx
+    )
+)
 ROWS = 88
 
 
 def kernel(
     own_hbm, idx_hbm, cls_hbm, brick_hbm, sel_hbm, img_hbm, slope_hbm, shape_hbm, nodes_hbm, gram_hbm,
     own_ref, idx_ref, cls_ref, brick_ref, sel_ref, img_ref, slope_ref, shape_ref, loaded,
-    t0, t1, merged, t2, tgt, lhs, wide, send_line, recv_line, send, recv, acc,
+    ask_out, ask_in, tgt, lhs, wide, send, recv, acc,
     gram, nodes, part, face_in, lid_in, edge_in,
-    s1, r1, s2, r2, sl, rl, ss, rs, hs, hr, stored,
+    asked, asks, ss, rs, hs, hr, stored,
 ):
     a = lax.axis_index("gz")
     b = lax.axis_index("xy")
@@ -101,8 +110,7 @@
     x_up = [lax.rem(x + d, 4) for d in range(4)]
     y_up = [lax.rem(y + d, 4) for d in range(4)]
     z_up = [lax.rem(z + d, 4) for d in range(4)]
-    line = [(core[p // 4], y * 16 + z * 4 + x_up[p % 4]) for p in range(8)]
-    plane = [(a, y_up[q // 4] * 16 + z_up[q % 4] * 4 + x) for q in range(16)]
+    x_down = [lax.rem(x + 4 - d, 4) for d in range(4)]
 
     loads = []
     for n, (src, dst) in enumerate(
@@ -121,8 +129,13 @@
     for n in range(5):
         loads[n].start()
     barrier = pltpu.get_barrier_semaphore()
-    for peer in line[1:] + plane[1:]:
-        pl.semaphore_signal(barrier, inc=1, device_id=peer, device_id_type=MESH)
+    for far, da, dy, dz, dx in FARTHEST_FIRST:
+        pl.semaphore_signal(
+            barrier,
+            inc=1,
+            device_id=(core[da], y_up[dy] * 16 + z_up[dz] * 4 + x_up[dx]),
+            device_id_type=MESH,
+        )
     for n in range(3):
         loads[n].wait()
 
@@ -135,9 +148,11 @@
     off_z = ((owner >> 2) - z) & 3
     off_x = (owner - x) & 3
     p_of = off_core * 4 + off_x
-    q_of = off_y * 4 + off_z
+    jy = (off_y - off_x) & 3
+    jz = (off_z - 2 * off_core - off_x) & 3
+    message = (jy * 2 + (jz >> 1)) * 16 + (jz & 1) * 8 + p_of
     sub = lax.broadcasted_iota(jnp.int32, (128, 512), 0)
-    hit = sub == p_of * 16 + q_of
+    hit = sub == message
     onehot = hit.astype(F32).astype(BF)
     before = (
         lax.broadcasted_iota(jnp.int32, (512, 512), 0)
@@ -145,10 +160,7 @@
     ).astype(F32).astype(BF)
     ahead = jnp.dot(onehot, before, preferred_element_type=F32)
     slot = jnp.sum(jnp.where(hit, ahead, 0.0), axis=0, keepdims=True).astype(jnp.int32)
-    jy = (off_y - off_x) & 3
-    jz = (off_z - 2 * off_core - off_x) & 3
-    message = (jy * 2 + (jz >> 1)) * 16 + (jz & 1) * 8 + p_of
-    target = jnp.where(q_of == 0, LINE + p_of, message) * CAP + slot
+    target = message * CAP + slot
     tgt[...] = jnp.broadcast_to(target, (128, 512)).T
     in_slot = (sub & 15) == slot
     low = jnp.where(in_slot, wanted & 255, 0).astype(F32).astype(BF)
@@ -157,19 +169,56 @@
         onehot, jnp.concatenate([low, high], axis=0), NT, preferred_element_type=F32
     )
     table = (table[:, :128] + 256.0 * table[:, 128:]).astype(jnp.int32)
-    group = lax.broadcasted_iota(jnp.int32, (128, 128), 0) >> 4
+    group = lax.broadcasted_iota(jnp.int32, (128, 128), 0) & 7
     lane = lax.broadcasted_iota(jnp.int32, (128, 128), 1)
-    t0[...] = jnp.where((lane >> 4) == group, table, 0).reshape(8, 16, 128)
-
-    pl.semaphore_wait(barrier, 22)
-    first = []
-    for p in range(1, 8):
-        copy = pltpu.make_async_remote_copy(
-            t0.at[p], t1.at[p], s1.at[p], r1.at[p], device_id=line[p], device_id_type=MESH
-        )
-        copy.start()
-        first.append(copy)
-    t1[0] = t0[0]
+    ask_out[...] = jnp.where((lane >> 4) == group, table, 0).reshape(16, 8, 128)
+
+    def offset(n, m):
+        dy = lax.rem(lax.div(n, 2) + m % 4, 4)
+        dz = lax.rem(2 * lax.rem(n, 2) + m // 8 + 2 * (m // 4 % 2) + m % 4, 4)
+        return dy, dz
+
+    def ask(n):
+        for m in range(16):
+            dy, dz = offset(n, m)
+            to = lax.rem(y + dy, 4) * 16 + lax.rem(z + dz, 4) * 4 + x_up[m % 4]
+
+            def go(m=m, to=to):
+                at = (2 * n + m // 8, pl.ds(m % 8, 1))
+                pltpu.make_async_remote_copy(
+                    ask_out.at[at],
+                    ask_in.at[at],
+                    asked.at[n],
+                    asks.at[n],
+                    device_id=(core[m // 4 % 2], to),
+                    device_id_type=MESH,
+                ).start()
+
+            if m:
+                go()
+            elif not isinstance(n, int):
+                pl.when(n > 0)(go)
+            elif n:
+                go()
+
+    def requests(n):
+        at = (pl.ds(2 * n, 2),)
+        return pltpu.make_async_remote_copy(
+            ask_out.at[at], ask_in.at[at], asked.at[n], asks.at[n],
+            device_id=(a, b), device_id_type=MESH,
+        )
+
+    def own_step():
+        at = (pl.ds(0, 15), pl.ds(0, 1))
+        return pltpu.make_async_remote_copy(
+            ask_out.at[at], ask_in.at[at], asked.at[0], asks.at[0],
+            device_id=(a, b), device_id_type=MESH,
+        )
+
+    ask_in[0, 0:1] = ask_out[0, 0:1]
+    pl.semaphore_wait(barrier, 127)
+    for n in range(4, 8):
+        ask(n)
     for n in range(5, 8):
         loads[n].start()
 
@@ -187,32 +236,13 @@
                 shift * 80 : shift * 80 + 80
             ]
 
-    for p in range(8):
-        jy, jz = -(p % 4) % 4, (-2 * (p // 4) - p % 4) % 4
-        recv[jy * 2 + jz // 2, jz % 2 * 8 + p] = jnp.zeros((ROWS, 128), BF)
     acc[...] = jnp.zeros_like(acc)
-    for copy in first:
-        copy.wait_recv()
-    rows = jnp.sum(t1[...], axis=0)
-    for q in range(16):
-        merged[q] = rows[q : q + 1]
-    t2[0] = rows[0:1]
-
-    def second(q, to=line[1]):
-        return pltpu.make_async_remote_copy(
-            merged.at[q], t2.at[q], s2.at[q], r2.at[q], device_id=to, device_id_type=MESH
-        )
-
-    for q in range(1, 16):
-        second(q, plane[q]).start()
 
     eye = (
         lax.broadcasted_iota(jnp.int32, (256, 256), 0)
         == lax.broadcasted_iota(jnp.int32, (256, 256), 1)
     ).astype(F32).astype(BF)
     half = lax.broadcasted_iota(jnp.int32, (8, 128), 1) < 64
-    slot_group = lax.broadcasted_iota(jnp.int32, (1, 128), 1) >> 4
-    x_down = [lax.rem(x + 4 - d, 4) for d in range(4)]
 
     def serve(request, out, post):
         width = request.shape[1]
@@ -276,53 +306,46 @@
             axis=1,
         )
 
-    on_line = [
-        pltpu.make_async_remote_copy(
-            send_line.at[p],
-            recv_line.at[p],
-            sl.at[p],
-            rl.at[p],
-            device_id=(core[p // 4], y * 16 + z * 4 + x_down[p % 4]),
-            device_id_type=MESH,
-        )
-        for p in range(1, 8)
-    ]
-    serve(t2[0], lambda m: send_line.at[m], lambda m: on_line[m - 1].start() if m else None)
-    recv_line[0] = send_line[0]
-    for q in range(1, 16):
-        second(q).wait_recv()
-
-    def all_of(n):
+    def all_of(n, lo):
+        part = pl.ds(lo, 16 - lo)
         return pltpu.make_async_remote_copy(
-            send.at[n, pl.ds(0, 15)], recv.at[n, pl.ds(0, 15)], ss.at[n], rs.at[n],
-            device_id=line[1], device_id_type=MESH,
+            send.at[n, part], recv.at[n, part], ss.at[n], rs.at[n],
+            device_id=(a, b), device_id_type=MESH,
         )
 
     def place(n):
-        all_of(n).wait_recv()
+        @pl.when(n == 0)
+        def _():
+            all_of(0, 1).wait_recv()
+
+        @pl.when(n > 0)
+        def _():
+            all_of(n, 0).wait_recv()
+
         rows = jnp.concatenate(
             [samples_of([recv.at[n, g * 8 + p] for p in range(8)]) for g in range(2)], axis=0
         )
         acc[...] += jnp.dot(pick_of(n * 256, 256), rows, preferred_element_type=F32)
 
-    def step(n, carry):
-        offsets = []
-        request = []
-        for g in range(2):
-            row = jnp.zeros((1, 128), jnp.int32)
-            for p in range(8):
-                dy = lax.rem(lax.div(n, 2) + p % 4, 4)
-                dz = lax.rem(2 * lax.rem(n, 2) + g + 2 * (p // 4) + p % 4, 4)
-                offsets.append((dy, dz))
-                row = jnp.where(slot_group == p, t2[dy * 4 + dz], row)
-            request.append(row)
+    def step(t, carry):
+        n = lax.rem(t + 4, 8)
+        pl.when(t < 4)(lambda: ask(t))
+
+        @pl.when(n == 0)
+        def _():
+            own_step().wait_recv()
+
+        @pl.when(n > 0)
+        def _():
+            requests(n).wait_recv()
+
+        request = [jnp.sum(ask_in[2 * n + g], axis=0, keepdims=True) for g in range(2)]
 
         def post(m):
-            dy, dz = offsets[m]
-
-            @pl.when(dy + dz > 0)
-            def _():
-                to = lax.rem(y + 4 - dy, 4) * 16 + lax.rem(z + 4 - dz, 4) * 4 + x_down[m % 4]
+            dy, dz = offset(n, m)
+            to = lax.rem(y + 4 - dy, 4) * 16 + lax.rem(z + 4 - dz, 4) * 4 + x_down[m % 4]
+
+            def go():
                 pltpu.make_async_remote_copy(
                     send.at[n, m],
                     recv.at[n, m],
@@ -332,22 +355,27 @@
                     device_id_type=MESH,
                 ).start()
 
+            if m:
+                go()
+            else:
+                pl.when(n > 0)(go)
+
         serve(jnp.concatenate(request, axis=1), lambda m: send.at[n, m], post)
 
-        @pl.when(n >= LAG)
+        @pl.when(n == 0)
         def _():
-            place(n - LAG)
+            recv[0, 0] = send[0, 0]
+
+        @pl.when(t >= LAG)
+        def _():
+            place(lax.rem(t + 4 - LAG, 8))
 
         return carry
 
     lax.fori_loop(0, 8, step, 0)
-    for p in range(1, 8):
-        on_line[p - 1].wait_recv()
-    rows = samples_of([recv_line.at[p] for p in range(8)])
-    acc[...] += jnp.dot(pick_of(LINE * CAP, 128), rows, preferred_element_type=F32)
-
-    def rest(n, carry):
-        place(n)
+
+    def rest(t, carry):
+        place(lax.rem(t + 4, 8))
         return carry
 
     lax.fori_loop(8 - LAG, 8, rest, 0)
@@ -441,13 +469,11 @@
     pl.when(b < 63)(to_face.wait_send)
     pl.when(a == 0)(to_lid.wait_send)
     pl.when((a == 0) & (b < 63))(to_edge.wait_send)
-    for p in range(1, 8):
-        first[p - 1].wait_send()
-        on_line[p - 1].wait_send()
-    for q in range(1, 16):
-        second(q).wait_send()
-    for n in range(8):
-        all_of(n).wait_send()
+    own_step().wait_send()
+    all_of(0, 1).wait_send()
+    for n in range(1, 8):
+        requests(n).wait_send()
+        all_of(n, 0).wait_send()
     for store in stores:
         store.wait()
 
@@ -493,15 +519,11 @@
             pltpu.VMEM((6, 512, 256), BF),
             pltpu.VMEM((160, 512), BF),
             dma((8,)),
-            pltpu.VMEM((8, 16, 128), jnp.int32),
-            pltpu.VMEM((8, 16, 128), jnp.int32),
-            pltpu.VMEM((16, 1, 128), jnp.int32),
-            pltpu.VMEM((16, 1, 128), jnp.int32),
+            pltpu.VMEM((16, 8, 128), jnp.int32),
+            pltpu.VMEM((16, 8, 128), jnp.int32),
             pltpu.VMEM((512, 128), jnp.int32),
             pltpu.VMEM((800, 2048), BF),
             pltpu.VMEM((768, 256), BF),
-            pltpu.VMEM((8, ROWS, 128), BF),
-            pltpu.VMEM((8, ROWS, 128), BF),
             pltpu.VMEM((8, 16, ROWS, 128), BF),
             pltpu.VMEM((8, 16, ROWS, 128), BF),
             pltpu.VMEM((512, 768), F32),
@@ -511,10 +533,6 @@
             pltpu.VMEM((4, 16, 128), F32),
             pltpu.VMEM((16, 128), F32),
             pltpu.VMEM((16, 128), F32),
-            dma((8,)),
-            dma((8,)),
-            dma((16,)),
-            dma((16,)),
             dma((8,)),
             dma((8,)),
             dma((8,)),

time: 64.2 us -> 62.1 us (0.967)
  Pallas kernels: 63.4 us -> 61.4 us
    pallas_call x1, Pallas kernels: 61.4 us -> 59.3 us  [run(): pl.pallas_call(kernel, out_shape=outs, in_specs=[hbm] * 8, out_specs=(hbm...]
where the time goes in v4:
time: 62.1 us; the launch traced here: 62 us
  Pallas kernels  61.4 us (99%)
  between operations  0.64 us (1%)
    pallas_call x1, Pallas kernels, run(): pl.pallas_call(kernel, out_shape=outs, in_specs=[hbm] * 8, out_specs=(hbm...  59.3 us
    pallas_call x1, Pallas kernels, run(): pl.pallas_call(copy_kernel, out_shape=outs, in_specs=[hbm] * 2, out_specs...  2.06 us

profile of v4, /device:TPU:9, one launch (start us, length us, event | category | flops | bytes accessed | tf_op | source)
XLA Modules:
  0.0 62.0 jit_solution(7551829379354804487)
XLA Ops:
  0.6 59.3 %shard_map.95 = (f32[9,4,1,128]{3,2,1,0:T(1,128)}, f32[4,576,128]{2,1,0:T(8,128)}) custom-call(s32[4,1,128]{2,1,0:T(1,128)} %bitcast.14, s32[4,1,128]{2,1,0:T(1,128)} %bitcast.15, s32[4,1,128]{2,1,0:T(1,128)} %bitcast.16, bf16[4,1000,128]{2,1,0:T(8,128)(2,1)} %bitcast.12, bf16[4,320,128]{2,1,0:T(8,128)(2,1)} %constant.6.clone.sel_hbm, ...), custom_call_target="tpu_custom_call" | custom-call | tf_op jit(solution)/shard_map/pallas_call | solution.py:507
  60.0 2.1 %shard_map.96 = (f32[9,4,1,128]{3,2,1,0:T(1,128)}, f32[4,576,128]{2,1,0:T(8,128)}) custom-call(f32[9,4,1,128]{3,2,1,0:T(1,128)} %get-tuple-element.6.nodes_in, f32[4,576,128]{2,1,0:T(8,128)} %get-tuple-element.7.gram_in), custom_call_target="tpu_custom_call" | custom-call | tf_op jit(solution)/shard_map/pallas_call | solution.py:557

commit v5 on v4

--- a/solution.py
+++ b/solution.py
@@ -217,11 +217,8 @@
 
     ask_in[0, 0:1] = ask_out[0, 0:1]
     pl.semaphore_wait(barrier, 127)
-    for n in range(4, 8):
+    for n in (4, 5, 6):
         ask(n)
-    for n in range(5, 8):
-        loads[n].start()
-
     loads[3].wait()
     loads[4].wait()
     for i in range(10):
@@ -235,6 +232,11 @@
             lhs[i * 80 : i * 80 + 80, shift * 512 : shift * 512 + 512] = picked[
                 shift * 80 : shift * 80 + 80
             ]
+
+    for n in (7, 0, 1, 2, 3):
+        ask(n)
+    for n in range(5, 8):
+        loads[n].start()
 
     acc[...] = jnp.zeros_like(acc)
 
@@ -329,8 +331,6 @@
 
     def step(t, carry):
         n = lax.rem(t + 4, 8)
-        pl.when(t < 4)(lambda: ask(t))
-
         @pl.when(n == 0)
         def _():
             own_step().wait_recv()

time: 62.1 us -> 61.9 us (level)
  no operation moved by 1% of the time
where the time goes in v5:
time: 61.9 us; the launch traced here: 61.8 us
  Pallas kernels  61.1 us (99%)
  between operations  0.64 us (1%)
    pallas_call x1, Pallas kernels, run(): pl.pallas_call(kernel, out_shape=outs, in_specs=[hbm] * 8, out_specs=(hbm...  59.1 us
    pallas_call x1, Pallas kernels, run(): pl.pallas_call(copy_kernel, out_shape=outs, in_specs=[hbm] * 2, out_specs...  2.06 us

profile of v5, /device:TPU:9, one launch (start us, length us, event | category | flops | bytes accessed | tf_op | source)
XLA Modules:
  0.0 61.8 jit_solution(2474106696641565455)
XLA Ops:
  0.6 59.1 %shard_map.95 = (f32[9,4,1,128]{3,2,1,0:T(1,128)}, f32[4,576,128]{2,1,0:T(8,128)}) custom-call(s32[4,1,128]{2,1,0:T(1,128)} %bitcast.14, s32[4,1,128]{2,1,0:T(1,128)} %bitcast.15, s32[4,1,128]{2,1,0:T(1,128)} %bitcast.16, bf16[4,1000,128]{2,1,0:T(8,128)(2,1)} %bitcast.12, bf16[4,320,128]{2,1,0:T(8,128)(2,1)} %constant.6.clone.sel_hbm, ...), custom_call_target="tpu_custom_call" | custom-call | tf_op jit(solution)/shard_map/pallas_call | solution.py:507
  59.7 2.1 %shard_map.96 = (f32[9,4,1,128]{3,2,1,0:T(1,128)}, f32[4,576,128]{2,1,0:T(8,128)}) custom-call(f32[9,4,1,128]{3,2,1,0:T(1,128)} %get-tuple-element.6.nodes_in, f32[4,576,128]{2,1,0:T(8,128)} %get-tuple-element.7.gram_in), custom_call_target="tpu_custom_call" | custom-call | tf_op jit(solution)/shard_map/pallas_call | solution.py:557

commit v6 on v5

--- a/solution.py
+++ b/solution.py
@@ -30,28 +30,25 @@
     return bf16_const(table)
 
 
-BLOCKS = ((0, 1), (1, 2), (0, 2), (1, 2), (0, 2), (1, 2))
+BLOCKS = ((0, 2), (1, 2), (0, 2), (1, 2))
 
 
 def slope_table():
     def at(i, j, k):
-        if i == 8:
-            return 640 + j * 8 + k
         if k == 8:
             return 512 + i * 16 + j
         if j == 8:
             return 512 + i * 16 + 8 + k
         return i * 64 + j * 8 + k
 
-    table = np.zeros((768, 1536), np.float32)
+    table = np.zeros((768, 1024), np.float32)
     for i in range(8):
         for j in range(8):
             for k in range(8):
                 v = at(i, j, k)
-                for c, up in enumerate((at(i + 1, j, k), at(i, j + 1, k), at(i, j, k + 1))):
+                for c, up in enumerate((at(i, j + 1, k), at(i, j, k + 1))):
                     table[up, c * 512 + v] = 1.0
                     table[v, c * 512 + v] = -1.0
-    table[704:] = table[640:704]
     blocks = []
     for n, (one, two) in enumerate(BLOCKS):
         columns = table[:, n * 256 : n * 256 + 256]
@@ -77,8 +74,11 @@
         rows.append((az[:, None, None] * ax[None, :, None] * ay[None, None, :]).reshape(512))
     shape = np.stack(rows)
     full = (shape[:, None, :] * shape[None, :, :]).reshape(64, 512) / 64.0
-    square = shape * shape / 64.0
-    return np.concatenate([split_rows(full), split_rows(square), split_rows(shape / 64.0)], axis=0)
+    table = np.zeros((2048, 128), ml_dtypes.bfloat16)
+    table[:512] = split_rows(full).T
+    for c in range(3):
+        table[512 + c * 512 : 1024 + c * 512, c * 16 : c * 16 + 16] = split_rows(shape / 64.0).T
+    return table
 
 
 PAIRS = ((0, 0), (0, 1), (0, 2), (1, 1), (1, 2), (2, 2))
@@ -201,6 +201,10 @@
             elif n:
                 go()
 
+    def ask_step(t, carry):
+        ask(lax.rem(t, 8))
+        return carry
+
     def requests(n):
         at = (pl.ds(2 * n, 2),)
         return pltpu.make_async_remote_copy(
@@ -217,8 +221,7 @@
 
     ask_in[0, 0:1] = ask_out[0, 0:1]
     pl.semaphore_wait(barrier, 127)
-    for n in (4, 5, 6):
-        ask(n)
+    lax.fori_loop(4, 7, ask_step, 0)
     loads[3].wait()
     loads[4].wait()
     for i in range(10):
@@ -233,8 +236,7 @@
                 shift * 80 : shift * 80 + 80
             ]
 
-    for n in (7, 0, 1, 2, 3):
-        ask(n)
+    lax.fori_loop(7, 12, ask_step, 0)
     for n in range(5, 8):
         loads[n].start()
 
@@ -383,16 +385,28 @@
     for n in range(5, 8):
         loads[n].wait()
     lane = lax.broadcasted_iota(jnp.int32, (8, 128), 1)
-    sums_of = [[None] * 5, [None] * 5]
-    stores = []
-
-    def add(old, new):
-        return new if old is None else [u + v for u, v in zip(old, new)]
-
-    for e in range(4):
-        w = acc[e * 128 : e * 128 + 128, :].astype(BF)
-        blocks = [w[:, n * 256 : n * 256 + 256] for n in range(3)]
+    node = lax.broadcasted_iota(jnp.int32, (8, 128), 0)
+    low = lax.broadcasted_iota(jnp.int32, (128, 128), 1) < 64
+    part[...] = jnp.zeros_like(part)
+
+    def store(e):
+        return pltpu.make_async_copy(gram.at[e], gram_hbm.at[e], stored.at[e])
+
+    def finish(e, carry):
+        here = pl.ds(e * 128, 128)
+        w = acc[here, :]
+        image = img_ref[here, :].astype(F32)
+        tiles = [w[:, n * 128 : n * 128 + 128] for n in range(4)]
+        turned = [pltpu.roll(tile, 64, 1) for tile in tiles]
+        last = w[:, 640:768]
+        turned.append(last + pltpu.roll(last, 64, 1))
         g = [
+            jnp.concatenate(
+                [jnp.where(low, turned[n], turned[n + 1]) - tiles[n] for n in range(4)], axis=1
+            )
+        ]
+        blocks = [w[:, n * 256 : n * 256 + 256].astype(BF) for n in range(3)]
+        halves = [
             jnp.dot(
                 jnp.concatenate([blocks[one], blocks[two]], axis=1),
                 slope_ref[n],
@@ -400,37 +414,41 @@
             )
             for n, (one, two) in enumerate(BLOCKS)
         ]
-        g = [jnp.concatenate(g[2 * c : 2 * c + 2], axis=1) for c in range(3)]
-        r = acc[e * 128 : e * 128 + 128, :512] - img_ref[e * 128 : e * 128 + 128, :].astype(F32)
+        g += [jnp.concatenate(halves[2 * c : 2 * c + 2], axis=1) for c in range(2)]
+        r = w[:, :512] - image
         products = jnp.concatenate([(g[c] * g[d]).astype(BF) for c, d in PAIRS], axis=0)
-        forces = jnp.concatenate([(g[c] * r).astype(BF) for c in range(3)], axis=0)
-        sums = lax.dot_general(shape_ref[:144, :], products, NT, preferred_element_type=F32)
-        full = sums[:64] + sums[64:128]
+        forces = jnp.concatenate([(g[c] * r).astype(BF) for c in range(3)], axis=1)
+        sums = jnp.dot(products, shape_ref[:512, :], preferred_element_type=F32)
+        full = []
+        for c in range(6):
+            by_node = sums[c * 128 : c * 128 + 128, :].T
+            full.append(by_node[:64] + by_node[64:])
+        force = jnp.dot(forces, shape_ref[512:, :], preferred_element_type=F32).T
         for c in range(3):
             for d in range(3):
-                at = PAIRS.index((min(c, d), max(c, d))) * 128
+                at = PAIRS.index((min(c, d), max(c, d)))
                 for n in range(8):
                     row = (c * 8 + n) * 24 + d * 8
-                    gram[e, row : row + 8, :] = full[n * 8 : n * 8 + 8, at : at + 128]
-        stores.append(pltpu.make_async_copy(gram.at[e], gram_hbm.at[e], stored.at[e]))
-        stores[-1].start()
-        square = sums[128:136] + sums[136:144]
-        force = lax.dot_general(shape_ref[144:160, :], forces, NT, preferred_element_type=F32)
-        force = force[:8] + force[8:]
-        terms = [force[:, c * 128 : c * 128 + 128] for c in range(3)]
-        terms += [square[:, c * 128 : c * 128 + 128] for c in range(6)]
+                    gram[e, row : row + 8, :] = full[at][n * 8 : n * 8 + 8]
+        store(e).start()
+        terms = [force[c * 16 : c * 16 + 8] + force[c * 16 + 8 : c * 16 + 16] for c in range(3)]
+        for c in range(6):
+            diagonal = full[c][0:8]
+            for n in range(1, 8):
+                diagonal = jnp.where(node == n, full[c][n * 8 : n * 8 + 8], diagonal)
+            terms.append(diagonal)
         both = []
         for t in terms:
             moved = jnp.where(lane == 0, 0.0, pltpu.roll(t, 1, 1))
             both.append(t + pltpu.roll(moved, 7, 0))
         for nx in range(2):
-            sums_of[nx][e] = add(sums_of[nx][e], [t[2 * nx : 2 * nx + 1] for t in both])
-            sums_of[nx][e + 1] = [t[4 + 2 * nx : 5 + 2 * nx] for t in both]
-    part[...] = jnp.zeros_like(part)
-    for nx in range(2):
-        for e in range(5):
             for c in range(9):
-                part[nx, e, c : c + 1, :] = sums_of[nx][e][c]
+                part[nx, e, c : c + 1, :] += both[c][2 * nx : 2 * nx + 1]
+                part[nx, e + 1, c : c + 1, :] = both[c][4 + 2 * nx : 5 + 2 * nx]
+        return carry
+
+    for e in range(4):
+        finish(e, 0)
 
     right = lax.rem(b + 1, 64)
     to_face = pltpu.make_async_remote_copy(
@@ -464,8 +482,8 @@
     for e in range(4):
         for c in range(9):
             nodes[c, e] = part[0, e, c : c + 1, :]
-    stores.append(pltpu.make_async_copy(nodes, nodes_hbm, stored.at[4]))
-    stores[-1].start()
+    store_nodes = pltpu.make_async_copy(nodes, nodes_hbm, stored.at[4])
+    store_nodes.start()
     pl.when(b < 63)(to_face.wait_send)
     pl.when(a == 0)(to_lid.wait_send)
     pl.when((a == 0) & (b < 63))(to_edge.wait_send)
@@ -474,8 +492,9 @@
     for n in range(1, 8):
         requests(n).wait_send()
         all_of(n, 0).wait_send()
-    for store in stores:
-        store.wait()
+    for e in range(4):
+        store(e).wait()
+    store_nodes.wait()
 
 
 def copy_kernel(nodes_in, gram_in, nodes_out, gram_out, nodes, gram, came, went):
@@ -516,8 +535,8 @@
             pltpu.VMEM((4, 1000, 128), BF),
             pltpu.VMEM((4, 320, 128), BF),
             pltpu.VMEM((512, 512), BF),
-            pltpu.VMEM((6, 512, 256), BF),
-            pltpu.VMEM((160, 512), BF),
+            pltpu.VMEM((4, 512, 256), BF),
+            pltpu.VMEM((2048, 128), BF),
             dma((8,)),
             pltpu.VMEM((16, 8, 128), jnp.int32),
             pltpu.VMEM((16, 8, 128), jnp.int32),

time: 61.9 us -> 61.5 us (level)
  no operation moved by 1% of the time
where the time goes in v6:
time: 61.5 us; the launch traced here: 61.4 us
  Pallas kernels  60.7 us (99%)
  between operations  0.64 us (1%)
    pallas_call x1, Pallas kernels, run(): pl.pallas_call(kernel, out_shape=outs, in_specs=[hbm] * 8, out_specs=(hbm...  58.7 us
    pallas_call x1, Pallas kernels, run(): pl.pallas_call(copy_kernel, out_shape=outs, in_specs=[hbm] * 2, out_specs...  2.06 us

profile of v6, /device:TPU:9, one launch (start us, length us, event | category | flops | bytes accessed | tf_op | source)
XLA Modules:
  0.0 61.4 jit_solution(5556448831443048670)
XLA Ops:
  0.6 58.7 %shard_map.95 = (f32[9,4,1,128]{3,2,1,0:T(1,128)}, f32[4,576,128]{2,1,0:T(8,128)}) custom-call(s32[4,1,128]{2,1,0:T(1,128)} %bitcast.14, s32[4,1,128]{2,1,0:T(1,128)} %bitcast.15, s32[4,1,128]{2,1,0:T(1,128)} %bitcast.16, bf16[4,1000,128]{2,1,0:T(8,128)(2,1)} %bitcast.12, bf16[4,320,128]{2,1,0:T(8,128)(2,1)} %constant.6.clone.sel_hbm, ...), custom_call_target="tpu_custom_call" | custom-call | tf_op jit(solution)/shard_map/pallas_call | solution.py:526
  59.3 2.1 %shard_map.96 = (f32[9,4,1,128]{3,2,1,0:T(1,128)}, f32[4,576,128]{2,1,0:T(8,128)}) custom-call(f32[9,4,1,128]{3,2,1,0:T(1,128)} %get-tuple-element.6.nodes_in, f32[4,576,128]{2,1,0:T(8,128)} %get-tuple-element.7.gram_in), custom_call_target="tpu_custom_call" | custom-call | tf_op jit(solution)/shard_map/pallas_call | solution.py:576

commit v7 on v6

--- a/solution.py
+++ b/solution.py
@@ -99,7 +99,7 @@
 def kernel(
     own_hbm, idx_hbm, cls_hbm, brick_hbm, sel_hbm, img_hbm, slope_hbm, shape_hbm, nodes_hbm, gram_hbm,
     own_ref, idx_ref, cls_ref, brick_ref, sel_ref, img_ref, slope_ref, shape_ref, loaded,
-    ask_out, ask_in, tgt, lhs, wide, send, recv, acc,
+    earlier, ask_out, ask_in, tgt, lhs, wide, send, recv, acc,
     gram, nodes, part, face_in, lid_in, edge_in,
     asked, asks, ss, rs, hs, hr, stored,
 ):
@@ -126,7 +126,7 @@
         )
     ):
         loads.append(pltpu.make_async_copy(src, dst, loaded.at[n]))
-    for n in range(5):
+    for n in range(3):
         loads[n].start()
     barrier = pltpu.get_barrier_semaphore()
     for far, da, dy, dz, dx in FARTHEST_FIRST:
@@ -136,6 +136,13 @@
             device_id=(core[da], y_up[dy] * 16 + z_up[dz] * 4 + x_up[dx]),
             device_id_type=MESH,
         )
+    for n in range(3, 5):
+        loads[n].start()
+    before = (
+        lax.broadcasted_iota(jnp.int32, (512, 512), 0)
+        < lax.broadcasted_iota(jnp.int32, (512, 512), 1)
+    ).astype(F32).astype(BF)
+    earlier[...] = before
     for n in range(3):
         loads[n].wait()
 
@@ -154,11 +161,7 @@
     sub = lax.broadcasted_iota(jnp.int32, (128, 512), 0)
     hit = sub == message
     onehot = hit.astype(F32).astype(BF)
-    before = (
-        lax.broadcasted_iota(jnp.int32, (512, 512), 0)
-        < lax.broadcasted_iota(jnp.int32, (512, 512), 1)
-    ).astype(F32).astype(BF)
-    ahead = jnp.dot(onehot, before, preferred_element_type=F32)
+    ahead = jnp.dot(onehot, earlier[...], preferred_element_type=F32)
     slot = jnp.sum(jnp.where(hit, ahead, 0.0), axis=0, keepdims=True).astype(jnp.int32)
     target = message * CAP + slot
     tgt[...] = jnp.broadcast_to(target, (128, 512)).T
@@ -391,6 +394,8 @@
 
     def store(e):
         return pltpu.make_async_copy(gram.at[e], gram_hbm.at[e], stored.at[e])
+
+    fulls = []
 
     def finish(e, carry):
         here = pl.ds(e * 128, 128)
@@ -424,13 +429,7 @@
             by_node = sums[c * 128 : c * 128 + 128, :].T
             full.append(by_node[:64] + by_node[64:])
         force = jnp.dot(forces, shape_ref[512:, :], preferred_element_type=F32).T
-        for c in range(3):
-            for d in range(3):
-                at = PAIRS.index((min(c, d), max(c, d)))
-                for n in range(8):
-                    row = (c * 8 + n) * 24 + d * 8
-                    gram[e, row : row + 8, :] = full[at][n * 8 : n * 8 + 8]
-        store(e).start()
+        fulls.append(full)
         terms = [force[c * 16 : c * 16 + 8] + force[c * 16 + 8 : c * 16 + 16] for c in range(3)]
         for c in range(6):
             diagonal = full[c][0:8]
@@ -463,6 +462,15 @@
     pl.when(b < 63)(to_face.start)
     pl.when(a == 0)(to_lid.start)
     pl.when((a == 0) & (b < 63))(to_edge.start)
+
+    for e in range(4):
+        for c in range(3):
+            for d in range(3):
+                at = PAIRS.index((min(c, d), max(c, d)))
+                for n in range(8):
+                    row = (c * 8 + n) * 24 + d * 8
+                    gram[e, row : row + 8, :] = fulls[e][at][n * 8 : n * 8 + 8]
+        store(e).start()
 
     @pl.when(b > 0)
     def _():
@@ -538,6 +546,7 @@
             pltpu.VMEM((4, 512, 256), BF),
             pltpu.VMEM((2048, 128), BF),
             dma((8,)),
+            pltpu.VMEM((512, 512), BF),
             pltpu.VMEM((16, 8, 128), jnp.int32),
             pltpu.VMEM((16, 8, 128), jnp.int32),
             pltpu.VMEM((512, 128), jnp.int32),

time: 61.5 us -> 61.5 us (level)
  no operation moved by 1% of the time
where the time goes in v7:
time: 61.5 us; the launch traced here: 61.4 us
  Pallas kernels  60.7 us (99%)
  between operations  0.64 us (1%)
    pallas_call x1, Pallas kernels, run(): pl.pallas_call(kernel, out_shape=outs, in_specs=[hbm] * 8, out_specs=(hbm...  58.7 us
    pallas_call x1, Pallas kernels, run(): pl.pallas_call(copy_kernel, out_shape=outs, in_specs=[hbm] * 2, out_specs...  2.06 us

profile of v7, /device:TPU:9, one launch (start us, length us, event | category | flops | bytes accessed | tf_op | source)
XLA Modules:
  0.0 61.4 jit_solution(3493619197938239110)
XLA Ops:
  0.6 58.7 %shard_map.95 = (f32[9,4,1,128]{3,2,1,0:T(1,128)}, f32[4,576,128]{2,1,0:T(8,128)}) custom-call(s32[4,1,128]{2,1,0:T(1,128)} %bitcast.14, s32[4,1,128]{2,1,0:T(1,128)} %bitcast.15, s32[4,1,128]{2,1,0:T(1,128)} %bitcast.16, bf16[4,1000,128]{2,1,0:T(8,128)(2,1)} %bitcast.12, bf16[4,320,128]{2,1,0:T(8,128)(2,1)} %constant.6.clone.sel_hbm, ...), custom_call_target="tpu_custom_call" | custom-call | tf_op jit(solution)/shard_map/pallas_call | solution.py:534
  59.3 2.1 %shard_map.96 = (f32[9,4,1,128]{3,2,1,0:T(1,128)}, f32[4,576,128]{2,1,0:T(8,128)}) custom-call(f32[9,4,1,128]{3,2,1,0:T(1,128)} %get-tuple-element.6.nodes_in, f32[4,576,128]{2,1,0:T(8,128)} %get-tuple-element.7.gram_in), custom_call_target="tpu_custom_call" | custom-call | tf_op jit(solution)/shard_map/pallas_call | solution.py:585
